TPU v7x, 512 devices: a whole 4x4x16 slice. The times are simulated.
512 devices in a mesh: serve: 64 (over z, y), tensor: 8 (over x, core).
Axes of the slice: x: 4, y: 4, z: 16, core: 2. Of those that a mesh axis runs over, the one named last changes fastest.
Arguments:
- queries: bfloat16 [256, 4, 56, 128], P('serve', None, 'tensor'), may hold values from -4.5 to 4.5
- new_keys: bfloat16 [256, 4, 8, 128], P('serve', None, 'tensor'), may hold values from -4.5 to 4.5
- new_values: bfloat16 [256, 4, 8, 128], P('serve', None, 'tensor'), may hold values from -6 to 6
- key_cache: bfloat16 [2304, 256, 8, 128], P('serve', None, 'tensor'), may hold values from -4.5 to 4.5
- value_cache: bfloat16 [2304, 256, 8, 128], P('serve', None, 'tensor'), may hold values from -6 to 6
- lengths: int32 [256], P('serve'), may hold values from 1 to 8448, as said below
- block_owner: int32 [2304], P('serve'), may hold values from 0 to 255, as said below
- block_number: int32 [2304], P('serve'), may hold values from 0 to 32
Outputs:
- attended: bfloat16 [1024, 7168], P(('serve', 'tensor'))
Inputs may be any that keep to these rules, and one draw needn't show every extreme that they name: `lengths`: the 4 sequences of each index of serve hold exactly one longer than 256, of length above 8192; the others are at most 256. Pool block p holds positions block_number[p] * 256 onward of sequence block_owner[p]. Each block 0 to ceil(length / 256) - 1 of every sequence is in the pool exactly once, and every pool block is such a block. Block 0 of a sequence lies on the index of serve that holds the sequence; a block on any other index belongs to the long sequence of the index that holds it, and each index holds at most one block of any other index's long sequence.
All inputs are finite; a program needn't handle non-finite values.
Results may differ from a plain program's by a relative error of at most 0.005.
Values may be sent and summed in bfloat16 or wider, within the bound.
No kernel may reach another device: no remote copies, remote signals or barrier semaphores. Data moves between devices by JAX's collectives and lax.ppermute only.
A program may use at most 64 MiB of HBM per device.

v0:
```python
import jax
import jax.numpy as jnp
from jax import lax
from jax.sharding import PartitionSpec as P

neg_fill = -1e30


def block_partial(query_rows, keys, values, visible, score_scale):
    scores = (
        jnp.einsum("bskgh,btkh->bkgst", query_rows, keys, preferred_element_type=jnp.float32)
        * score_scale
    )
    scores = jnp.where(visible, scores, neg_fill)
    block_top = jnp.max(scores, axis=-1)
    weights = jnp.where(visible, jnp.exp(scores - block_top[..., None]), 0.0).astype(jnp.bfloat16)
    block_sum = jnp.sum(weights.astype(jnp.float32), axis=-1)
    block_out = jnp.einsum("bkgst,btkh->bkgsh", weights, values, preferred_element_type=jnp.float32)
    return (block_top, block_sum, block_out)


def shards(
    queries, new_keys, new_values, key_cache, value_cache, lengths, block_owner, block_number
):
    seq_dev, step_count, query_heads, head_dim = queries.shape
    pool_dev, block_span, kv_heads, unused_dim = key_cache.shape
    groups = query_heads // kv_heads
    devices = lax.axis_size("serve")
    my_index = lax.axis_index("serve")
    score_scale = head_dim ** (-0.5)
    own_query = queries.reshape(seq_dev, step_count, kv_heads, groups, head_dim)
    owner_dev = block_owner // seq_dev
    own_slot = block_owner % seq_dev
    is_local = owner_dev == my_index
    is_long = lengths > block_span
    long_index = jnp.sum(jnp.where(is_long, jnp.arange(seq_dev, dtype=jnp.int32), 0))
    long_length = jnp.sum(jnp.where(is_long, lengths, 0)).reshape(1)
    positions = (
        block_number[:, None] * block_span + jnp.arange(block_span, dtype=jnp.int32)[None, :]
    )
    segment = jnp.where(is_local, own_slot, seq_dev + owner_dev)
    onehot = segment[:, None] == jnp.arange(seq_dev + devices, dtype=jnp.int32)[None, :]
    member = onehot.astype(jnp.float32)
    long_mask = is_long[:, None, None, None]
    long_rows = lax.dynamic_slice_in_dim(own_query, long_index, 1, 0)
    far_rows = lax.all_gather(long_rows, "serve", axis=0, tiled=True)
    far_length = lax.all_gather(long_length, "serve", axis=0, tiled=True)
    query_rows = jnp.where(
        is_local[:, None, None, None, None],
        jnp.take(own_query, own_slot, axis=0),
        jnp.take(far_rows, owner_dev, axis=0),
    )
    length_of = jnp.where(is_local, jnp.take(lengths, own_slot), jnp.take(far_length, owner_dev))
    visible = (positions < length_of[:, None])[:, None, None, None, :]
    block_top, block_sum, block_out = block_partial(
        query_rows, key_cache, value_cache, visible, score_scale
    )
    seg_top = jnp.max(
        jnp.where(onehot[:, :, None, None, None], block_top[:, None], neg_fill), axis=0
    )
    factor = jnp.exp(block_top - jnp.take(seg_top, segment, axis=0))
    seg_sum = jnp.einsum(
        "pn,pkgs->nkgs", member, factor * block_sum, precision=lax.Precision.HIGHEST
    )
    seg_out = jnp.einsum(
        "pn,pkgsh->nkgsh", member, factor[..., None] * block_out, precision=lax.Precision.HIGHEST
    )
    remote_top = seg_top[seq_dev:]
    remote_sum = seg_sum[seq_dev:]
    remote_out = seg_out[seq_dev:]
    back_top = lax.all_to_all(remote_top, "serve", split_axis=0, concat_axis=0, tiled=True)
    back_sum = lax.all_to_all(remote_sum, "serve", split_axis=0, concat_axis=0, tiled=True)
    back_out = lax.all_to_all(remote_out, "serve", split_axis=0, concat_axis=0, tiled=True)
    got_top = jnp.max(back_top, axis=0, keepdims=True)
    rescale = jnp.exp(back_top - got_top)
    got_sum = jnp.sum(back_sum * rescale, axis=0, keepdims=True)
    got_out = jnp.sum(back_out * rescale[..., None], axis=0, keepdims=True)
    causal = jnp.arange(step_count)[None, :] <= jnp.arange(step_count)[:, None]
    new_top, new_sum, new_out = block_partial(
        own_query, new_keys, new_values, causal[None, None, None], score_scale
    )
    near_top = seg_top[:seq_dev]
    far_top = jnp.where(long_mask, got_top, neg_fill)
    overall = jnp.maximum(jnp.maximum(near_top, new_top), far_top)
    near_factor = jnp.exp(near_top - overall)
    new_factor = jnp.exp(new_top - overall)
    far_factor = jnp.where(long_mask, jnp.exp(got_top - overall), 0.0)
    total = near_factor * seg_sum[:seq_dev] + new_factor * new_sum + far_factor * got_sum
    combined = (
        near_factor[..., None] * seg_out[:seq_dev]
        + new_factor[..., None] * new_out
        + far_factor[..., None] * got_out
    )
    result = combined / total[..., None]
    rows_out = jnp.transpose(result.astype(jnp.bfloat16), (0, 3, 1, 2, 4)).reshape(
        seq_dev * step_count, query_heads * head_dim
    )
    return lax.all_to_all(rows_out, "tensor", split_axis=0, concat_axis=1, tiled=True)


def solution(mesh):
    placed = (
        P("serve", None, "tensor", None),
        P("serve", None, "tensor", None),
        P("serve", None, "tensor", None),
        P("serve", None, "tensor", None),
        P("serve", None, "tensor", None),
        P("serve"),
        P("serve"),
        P("serve"),
    )
    return jax.shard_map(
        shards, mesh=mesh, in_specs=placed, out_specs=P(("serve", "tensor"), None), check_vma=False
    )
```

profile of v0, /device:TPU:1, one launch (start us, length us, event | category | flops | bytes accessed | tf_op | source)
XLA Modules:
  0.0 265.0 jit_solution(16072416630508840415)
XLA Ops:
  0.0 0.0 copy-start
  0.0 1.5 select_reduce_fusion.1
  1.5 1.5 fusion.51
  2.9 1.2 compare_and_fusion
  4.2 0.7 iota_compare_fusion
  4.8 0.0 copy-done.6
  4.8 0.6 compare_select_fusion
  7.3 0.7 constant_dynamic-slice_fusion
  8.0 81.3 %all-gather = bf16[64,4,7,128]{3,1,2,0:T(4,128)(2,1)S(1)} all-gather(bf16[1,4,7,128]{3,1,2,0:T(4,128)(2,1)S(1)} %constant_dynamic-slice_fusion), channel_id=2, replica_groups=mesh['serve'=64,'tensor'=8] {'serve'}, dimensions={0}, use_global_device_ids=true | all-gather | bytes 465920 | tf_op jit(solution)/shard_map/all_gather | solution.py:46
  89.3 1.5 gather_fusion.1
  90.9 1.3 dynamic-slice.4
  92.2 1.3 dynamic-update-slice
  93.5 19.8 %all-reduce = s32[64]{0:T(128)S(1)} all-reduce(s32[64]{0:T(128)S(1)} %dynamic-update-slice), channel_id=1, replica_groups=mesh['serve'=64,'tensor'=8] {'serve'}, use_global_device_ids=true, to_apply=%add | all-reduce | flops 64 | bytes 512
  113.2 0.8 gather_fusion.2
  114.0 0.8 gather_fusion
  114.8 0.0 copy-done.9
  114.8 2.5 fusion.47
  117.4 0.1 add_compare_fusion
  117.4 0.0 copy-start.4
  117.5 0.4 select_select_fusion
  117.8 0.0 copy-done
  117.8 1.6 fusion.52
  119.5 0.0 copy-done.4
  119.5 1.8 copy.55
  121.3 1.3 select_reduce_fusion
  122.6 0.0 copy-start.3
  122.6 0.8 copy.61
  123.4 1.3 pad_clamp_fusion
  124.6 2.0 convert_reduce_fusion
  126.6 2.3 gather_fusion.3
  128.9 1.7 fusion.50
  130.6 0.9 fusion.26
  131.5 0.6 copy-done.5
  132.1 0.7 slice_bitcast_fusion.1
  132.8 1.5 copy.71
  134.3 9.4 %all-to-all-start.2 = ((f32[64,1,7,4]{2,3,1,0:T(4,128)}), f32[64,1,7,4]{2,3,1,0:T(4,128)}, u32[]{:S(2)}, u32[]{:S(2)}) async-start(f32[64,1,7,4]{2,3,1,0:T(4,128)} %copy.71), calls=%async_computation.2 | async-start | bytes 262144 | tf_op jit(solution)/shard_map/all_to_all | solution.py:72
  143.7 0.0 copy-start.7
  143.7 2.4 fusion.16
  146.1 0.0 copy-done.7
  146.1 0.9 fusion.22
  147.0 0.1 slice_bitcast_fusion.2
  147.1 0.8 copy.59
  147.9 10.6 %all-to-all-done.2 = f32[64,1,7,4]{2,3,1,0:T(4,128)} async-done(((f32[64,1,7,4]{2,3,1,0:T(4,128)}), f32[64,1,7,4]{2,3,1,0:T(4,128)}, u32[]{:S(2)}, u32[]{:S(2)}) %all-to-all-start.2) | async-done | bytes 7200 | tf_op jit(solution)/shard_map/all_to_all | solution.py:72
  158.5 4.6 %all-to-all-start = ((f32[64,1,7,4]{2,3,1,0:T(4,128)}), f32[64,1,7,4]{2,3,1,0:T(4,128)S(1)}, u32[]{:S(2)}, u32[]{:S(2)}) async-start(f32[64,1,7,4]{2,3,1,0:T(4,128)} %copy.59), calls=%async_computation | async-start | bytes 262144 | tf_op jit(solution)/shard_map/all_to_all | solution.py:71
  163.1 0.1 slice_bitcast_fusion
  163.2 1.5 copy.67
  164.8 13.5 %all-to-all-done = f32[64,1,7,4]{2,3,1,0:T(4,128)S(1)} async-done(((f32[64,1,7,4]{2,3,1,0:T(4,128)}), f32[64,1,7,4]{2,3,1,0:T(4,128)S(1)}, u32[]{:S(2)}, u32[]{:S(2)}) %all-to-all-start) | async-done | bytes 7200 | tf_op jit(solution)/shard_map/all_to_all | solution.py:71
  178.3 5.5 %all-to-all-start.1 = ((f32[64,1,7,4,128]{4,3,2,1,0:T(4,128)}), f32[64,1,7,4,128]{4,3,2,1,0:T(4,128)}, u32[]{:S(2)}, u32[]{:S(2)}) async-start(f32[64,1,7,4,128]{4,3,2,1,0:T(4,128)} %copy.67), calls=%async_computation.1 | async-start | bytes 1835008 | tf_op jit(solution)/shard_map/all_to_all | solution.py:73
  183.8 2.1 fusion.53
  185.9 0.8 copy.58
  186.7 1.5 convert_reduce_fusion.1
  188.2 0.8 copy.70
  189.0 1.2 broadcast_compare_fusion
  190.2 1.7 fusion.40
  191.8 0.7 reduce_max.41
  192.5 2.2 fusion.25
  194.7 2.1 copy.68
  196.9 0.8 fusion.39
  197.7 19.0 %all-to-all-done.1 = f32[64,1,7,4,128]{4,3,2,1,0:T(4,128)} async-done(((f32[64,1,7,4,128]{4,3,2,1,0:T(4,128)}), f32[64,1,7,4,128]{4,3,2,1,0:T(4,128)}, u32[]{:S(2)}, u32[]{:S(2)}) %all-to-all-start.1) | async-done | bytes 917536 | tf_op jit(solution)/shard_map/all_to_all | solution.py:73
  216.7 1.8 multiply_reduce_fusion
  218.5 0.0 copy-done.2
  218.5 0.2 fusion.33
  218.7 45.6 %all_to_all.34 = bf16[8,2,896]{2,1,0:T(2,128)(2,1)S(1)} all-to-all(bf16[8,2,896]{2,1,0:T(2,128)(2,1)S(1)} %all_to_all.26), channel_id=1, replica_groups=mesh['serve'=64,'tensor'=8] {'tensor'}, dimensions={0} | all-to-all | bytes 57344 | tf_op jit(solution)/shard_map/all_to_all | solution.py:98
  264.3 0.6 copy.116
  (22 shorter events, 0.1 us)
Async XLA Ops:
  0.0 117.8 %copy-start = (bf16[36,256,1,128]{3,1,2,0:T(8,128)(2,1)S(1)}, bf16[36,256,1,128]{3,1,2,0:T(8,128)(2,1)}, u32[]{:S(2)}) copy-start(bf16[36,256,1,128]{3,1,2,0:T(8,128)(2,1)} %param.11) | copy-start | bytes 7077892
  0.0 114.8 %copy-start.9 = (s32[36]{0:T(128)S(1)}, s32[36]{0:T(128)}, u32[]{:S(2)}) copy-start(s32[36]{0:T(128)} %param.15) | copy-start | bytes 436
  4.2 0.7 copy-start.6
  117.4 2.0 copy-start.4
  122.6 24.4 %copy-start.3 = (f32[68,7,4]{0,2,1:T(4,128)}, f32[68,7,4]{0,2,1:T(4,128)S(1)}, u32[]{:S(2)}) copy-start(f32[68,7,4]{0,2,1:T(4,128)S(1)} %select_reduce_fusion) | copy-start | bytes 22852
  131.5 0.6 copy-start.5
  134.3 24.2 %all-to-all-start.2 = ((f32[64,1,7,4]{2,3,1,0:T(4,128)}), f32[64,1,7,4]{2,3,1,0:T(4,128)}, u32[]{:S(2)}, u32[]{:S(2)}) async-start(f32[64,1,7,4]{2,3,1,0:T(4,128)} %copy.71), calls=%async_computation.2 | async-start | bytes 262144 | tf_op jit(solution)/shard_map/all_to_all | solution.py:72
  143.7 2.4 copy-start.7
  158.5 19.8 %all-to-all-start = ((f32[64,1,7,4]{2,3,1,0:T(4,128)}), f32[64,1,7,4]{2,3,1,0:T(4,128)S(1)}, u32[]{:S(2)}, u32[]{:S(2)}) async-start(f32[64,1,7,4]{2,3,1,0:T(4,128)} %copy.59), calls=%async_computation | async-start | bytes 262144 | tf_op jit(solution)/shard_map/all_to_all | solution.py:71
  164.8 19.0 %copy-start.1 = (bf16[4,4,7,128]{3,1,2,0:T(4,128)(2,1)S(1)}, bf16[4,4,7,128]{3,1,2,0:T(4,128)(2,1)}, u32[]{:S(2)}) copy-start(bf16[4,4,7,128]{3,1,2,0:T(4,128)(2,1)} %param.8) | copy-start | bytes 86020
  178.3 38.4 %all-to-all-start.1 = ((f32[64,1,7,4,128]{4,3,2,1,0:T(4,128)}), f32[64,1,7,4,128]{4,3,2,1,0:T(4,128)}, u32[]{:S(2)}, u32[]{:S(2)}) async-start(f32[64,1,7,4,128]{4,3,2,1,0:T(4,128)} %copy.67), calls=%async_computation.1 | async-start | bytes 1835008 | tf_op jit(solution)/shard_map/all_to_all | solution.py:73
  183.8 3.0 %copy-start.8 = (pred[4,4]{1,0:T(4,128)(4,1)}, pred[4,4]{1,0:T(4,128)(4,1)S(1)}, u32[]{:S(2)}) copy-start(pred[4,4]{1,0:T(4,128)(4,1)S(1)} %iota_compare_fusion.3) | copy-start | bytes 52
  194.7 23.8 %copy-start.2 = (f32[4,7,4,128]{3,1,2,0:T(8,128)S(1)}, f32[4,7,4,128]{3,1,2,0:T(8,128)}, u32[]{:S(2)}) copy-start(f32[4,7,4,128]{3,1,2,0:T(8,128)} %fusion.40) | copy-start | bytes 172036
where the time goes:
time: 266 us; the launch traced here: 265 us
  blocking collectives  147 us (55%)
  waiting for transfers between devices  43.1 us (16%)
  local copies, waits for them, and re-layouts  22.5 us (8%)
  other arithmetic  21.5 us (8%)
  starting transfers between devices  19.5 us (7%)
  matrix products  9.61 us (4%)
    all_gather x1, blocking collectives, shards(): far_rows = lax.all_gather(long_rows, 'serve', axis=0, tiled=True)  81.3 us
    all_to_all x1, blocking collectives, shards(): lax.all_to_all(rows_out, 'tensor', split_axis=0, concat_axis=1, tiled=True)  45.6 us
    unnamed x1, blocking collectives  19.8 us
    all_to_all x1, waiting for transfers between devices, shards(): lax.all_to_all(remote_out, 'serve', split_axis=0, concat_axis=0, tiled=True)  19 us
    all_to_all x1, waiting for transfers between devices, shards(): lax.all_to_all(remote_top, 'serve', split_axis=0, concat_axis=0, tiled=True)  13.5 us
    all_to_all x1, waiting for transfers between devices, shards(): lax.all_to_all(remote_sum, 'serve', split_axis=0, concat_axis=0, tiled=True)  10.6 us
    all_to_all x1, starting transfers between devices, shards(): lax.all_to_all(remote_sum, 'serve', split_axis=0, concat_axis=0, tiled=True)  9.4 us
    all_to_all x1, starting transfers between devices, shards(): lax.all_to_all(remote_out, 'serve', split_axis=0, concat_axis=0, tiled=True)  5.48 us
  transfers between devices with their start and end apart: 3, of which 3 were waited for; matrix products, arithmetic and copies ran while one was open for 7% of the time, Pallas kernels for 0%

commit v1 on v0

v1 whole, which is shorter than its diff:
```python
import functools
import math

import jax
import jax.numpy as jnp
from jax import lax
from jax.experimental import pallas as pl
from jax.experimental.pallas import tpu as pltpu
from jax.sharding import PartitionSpec as P

neg_fill = -1e30
PAD = 32
F32 = jnp.float32
BF16 = jnp.bfloat16


def iota(shape, dim):
    return lax.broadcasted_iota(jnp.int32, shape, dim)


def prep_kernel(lengths, queries, own, message, padded):
    slots, groups, steps, head_dim = queries.shape
    rows = groups * steps
    long_slot = jnp.int32(0)
    for slot in range(slots):
        long_slot = long_slot + jnp.where(lengths[slot] > 256, slot, 0)
        length = lengths[slot]
        for g in range(groups):
            padded[slot, g * steps : (g + 1) * steps, :] = queries[slot, g].astype(F32)
        row = iota((PAD - rows, head_dim), 0)
        high = lax.shift_right_logical(length, 6).astype(F32)
        low = lax.bitwise_and(length, 63).astype(F32)
        padded[slot, rows:PAD, :] = jnp.where(row == 0, high, jnp.where(row == 1, low, 0.0))
        own[slot] = padded[slot].astype(BF16)
    tile = padded[long_slot].astype(BF16)
    message[...] = jnp.broadcast_to(tile[None], message.shape)


def main_kernel(
    chunk, scale2, owners, numbers, far, own, new_keys, new_values, key_cache, value_cache,
    back, local_out, local_lse,
    keys, values, block_out, block_lse, sems,
):
    blocks, span, head_dim = keys.shape
    slots = own.shape[0]
    steps = new_keys.shape[1]
    rows = 28
    me = lax.axis_index("serve")
    copies = []
    for c in range(blocks // chunk):
        part = pl.ds(c * chunk, chunk)
        pair = (
            pltpu.make_async_copy(key_cache.at[part], keys.at[part], sems.at[0, c]),
            pltpu.make_async_copy(value_cache.at[part], values.at[part], sems.at[1, c]),
        )
        for copy in pair:
            copy.start()
        copies.append(pair)

    row = iota((PAD, head_dim), 0)
    lane = iota((PAD, head_dim), 1)
    offset = lax.bitwise_and(me, 3) * PAD
    diagonal = jnp.logical_and(lane == offset + row, row < rows)
    in_span = jnp.logical_and(lane >= offset, lane < offset + rows)
    empty = jnp.where(jnp.logical_and(row == rows, in_span), neg_fill, 0.0).astype(BF16)
    back[...] = jnp.broadcast_to(empty[None], back.shape)

    all_rows = own[...].reshape(slots * PAD, head_dim)
    nk = new_keys[...].astype(F32).reshape(slots * steps, head_dim).astype(BF16)
    nv = new_values[...].astype(F32).reshape(slots * steps, head_dim).astype(BF16)
    scores = lax.dot_general(all_rows, nk, (((1,), (1,)), ((), ())), preferred_element_type=F32)
    r2, c2 = iota(scores.shape, 0), iota(scores.shape, 1)
    seen = jnp.logical_and(r2 // PAD == c2 // steps, c2 % steps <= r2 % steps)
    scores = jnp.where(seen, scores, neg_fill)
    top = jnp.max(scores, axis=1, keepdims=True)
    weights = jnp.where(seen, jnp.exp2((scores - top) * scale2), 0.0).astype(BF16)
    total = jnp.sum(weights.astype(F32), axis=1, keepdims=True)
    out = lax.dot_general(weights, nv, (((1,), (0,)), ((), ())), preferred_element_type=F32)
    out = out / total
    lse = jnp.broadcast_to(top * scale2 + jnp.log2(total), out.shape)
    local_out[...] = out.reshape(local_out.shape)
    local_lse[...] = lse.reshape(local_lse.shape)

    position = iota((PAD, span), 1)
    for c in range(blocks // chunk):
        for copy in copies[c]:
            copy.wait()
        ids = range(c * chunk, (c + 1) * chunk)
        owner = [owners[p] for p in ids]
        device = [lax.shift_right_logical(o, 2) for o in owner]
        mine = [d == me for d in device]
        raw = []
        for k, p in enumerate(ids):
            slot = lax.bitwise_and(owner[k], 3)
            query = jnp.where(mine[k], own[slot], far[device[k]])
            lens = query[rows : rows + 2, :].astype(F32)
            length = lens[0:1, 0:1] * 64.0 + lens[1:2, 0:1]
            score = lax.dot_general(
                query, keys[p], (((1,), (1,)), ((), ())), preferred_element_type=F32
            )
            limit = length - (numbers[p] * span).astype(F32)
            raw.append(jnp.where(position.astype(F32) < limit, score, neg_fill))
        raw = jnp.concatenate(raw, axis=0)
        top = jnp.max(raw, axis=1, keepdims=True)
        weights = jnp.exp2((raw - top) * scale2).astype(BF16)
        total = jnp.sum(weights.astype(F32), axis=1, keepdims=True)
        lse = top * scale2 + jnp.log2(total)
        inverse = 1.0 / total
        for k, p in enumerate(ids):
            part = slice(k * PAD, (k + 1) * PAD)
            out = lax.dot_general(
                weights[part], values[p], (((1,), (0,)), ((), ())), preferred_element_type=F32
            )
            out = out * inverse[part]
            column = jnp.broadcast_to(lse[part], out.shape)
            block_out[p] = out
            block_lse[p] = column
            flat = jnp.sum(jnp.where(diagonal, column, 0.0), axis=0, keepdims=True)
            high = flat.astype(BF16).astype(F32)
            rest = flat - high
            middle = rest.astype(BF16).astype(F32)
            low = rest - middle
            stats = jnp.where(
                row == rows,
                high,
                jnp.where(row == rows + 1, middle, jnp.where(row == rows + 2, low, 0.0)),
            )
            back[device[k]] = jnp.where(row < rows, out, stats).astype(BF16)
    back[me] = empty

    def merge(p, carry):
        owner = owners[p]

        @pl.when(lax.shift_right_logical(owner, 2) == me)
        def _():
            slot = lax.bitwise_and(owner, 3)
            old, new = local_lse[slot], block_lse[p]
            overall = jnp.maximum(old, new)
            a, b = jnp.exp2(old - overall), jnp.exp2(new - overall)
            total = a + b
            local_out[slot] = (a * local_out[slot] + b * block_out[p]) / total
            local_lse[slot] = overall + jnp.log2(total)

        return carry

    lax.fori_loop(0, blocks, merge, 0)


def combine_kernel(lengths, got, local_out, local_lse, result):
    devices, _, head_dim = got.shape
    slots = local_out.shape[0]
    steps, groups, rows = 4, 7, 28
    depth = devices * PAD
    many = devices // 4
    flat = got[...].reshape(depth, head_dim)
    g2, k2 = iota((many, depth), 0), iota((many, depth), 1)
    in_row = jnp.logical_and(k2 % PAD >= rows, k2 % PAD < rows + 3)
    pick = jnp.logical_and(k2 // (4 * PAD) == g2, in_row)
    lse = lax.dot_general(
        jnp.where(pick, 1.0, 0.0).astype(BF16), flat, (((1,), (0,)), ((), ())),
        preferred_element_type=F32,
    )
    top = jnp.max(lse, axis=0, keepdims=True)
    top = jnp.broadcast_to(top, (8, head_dim))
    top = jnp.maximum(top, pltpu.roll(top, 2 * PAD, 1))
    top = jnp.maximum(top, pltpu.roll(top, PAD, 1))
    weight = jnp.exp2(lse - top[0:1])
    row, lane = iota((PAD, head_dim), 0), iota((PAD, head_dim), 1)
    same = jnp.logical_and(lane % PAD == row, row < rows)
    spread = jnp.concatenate(
        [jnp.where(same, weight[g : g + 1], 0.0) for g in range(many)], axis=1
    )
    high = spread.astype(BF16)
    low = (spread - high.astype(F32)).astype(BF16)
    both = jnp.concatenate([high, low], axis=0)
    out = lax.dot_general(both, flat, (((1,), (0,)), ((), ())), preferred_element_type=F32)
    out = out[:PAD] + out[PAD:]
    total = jnp.sum(spread, axis=1, keepdims=True)
    total = jnp.where(row[:, 0:1] < rows, total, 1.0)
    first = jnp.logical_and(lane == row, row < rows)
    column = jnp.sum(jnp.where(first, top[0:1], 0.0), axis=1, keepdims=True)
    far_out = out / total
    far_lse = jnp.broadcast_to(column + jnp.log2(total), far_out.shape)
    for slot in range(slots):
        far_here = jnp.where(lengths[slot] > 256, far_lse, neg_fill)
        near = local_lse[slot]
        overall = jnp.maximum(far_here, near)
        a, b = jnp.exp2(far_here - overall), jnp.exp2(near - overall)
        final = ((a * far_out + b * local_out[slot]) / (a + b)).astype(BF16)
        for g in range(groups):
            result[slot * steps : (slot + 1) * steps, g * head_dim : (g + 1) * head_dim] = final[
                g * steps : (g + 1) * steps
            ]


VMEM = pl.BlockSpec(memory_space=pltpu.VMEM)
SMEM = pl.BlockSpec(memory_space=pltpu.SMEM)
ANY = pl.BlockSpec(memory_space=pl.ANY)


def shards(
    queries, new_keys, new_values, key_cache, value_cache, lengths, block_owner, block_number
):
    slots, steps, groups, head_dim = queries.shape
    blocks, span = key_cache.shape[:2]
    devices = lax.axis_size("serve")
    chunk = 6
    scale2 = head_dim**-0.5 * math.log2(math.e)
    queries = jnp.transpose(queries, (0, 2, 1, 3))
    new_keys = new_keys.reshape(slots, steps, head_dim)
    new_values = new_values.reshape(slots, steps, head_dim)
    key_cache = key_cache.reshape(blocks, span, head_dim)
    value_cache = value_cache.reshape(blocks, span, head_dim)

    own, message = pl.pallas_call(
        prep_kernel,
        out_shape=(
            jax.ShapeDtypeStruct((slots, PAD, head_dim), BF16),
            jax.ShapeDtypeStruct((devices, PAD, head_dim), BF16),
        ),
        in_specs=[SMEM, VMEM],
        out_specs=(VMEM, VMEM),
        scratch_shapes=[pltpu.VMEM((slots, PAD, head_dim), F32)],
        name="prep",
    )(lengths, queries)
    far = lax.all_to_all(message, "serve", split_axis=0, concat_axis=0, tiled=True)
    back, local_out, local_lse = pl.pallas_call(
        functools.partial(main_kernel, chunk, scale2),
        out_shape=(
            jax.ShapeDtypeStruct((devices, PAD, head_dim), BF16),
            jax.ShapeDtypeStruct((slots, PAD, head_dim), F32),
            jax.ShapeDtypeStruct((slots, PAD, head_dim), F32),
        ),
        in_specs=[SMEM, SMEM, VMEM, VMEM, VMEM, VMEM, ANY, ANY],
        out_specs=(VMEM, VMEM, VMEM),
        scratch_shapes=[
            pltpu.VMEM((blocks, span, head_dim), BF16),
            pltpu.VMEM((blocks, span, head_dim), BF16),
            pltpu.VMEM((blocks, PAD, head_dim), F32),
            pltpu.VMEM((blocks, PAD, head_dim), F32),
            pltpu.SemaphoreType.DMA((2, blocks // chunk)),
        ],
        compiler_params=pltpu.CompilerParams(vmem_limit_bytes=24 << 20),
        name="blocks",
    )(block_owner, block_number, far, own, new_keys, new_values, key_cache, value_cache)
    got = lax.all_to_all(back, "serve", split_axis=0, concat_axis=0, tiled=True)
    rows_out = pl.pallas_call(
        combine_kernel,
        out_shape=jax.ShapeDtypeStruct((slots * steps, groups * head_dim), BF16),
        in_specs=[SMEM, VMEM, VMEM, VMEM],
        out_specs=VMEM,
        name="combine",
    )(lengths, got, local_out, local_lse)
    return lax.all_to_all(rows_out, "tensor", split_axis=0, concat_axis=1, tiled=True)


def solution(mesh):
    placed = (
        P("serve", None, "tensor", None),
        P("serve", None, "tensor", None),
        P("serve", None, "tensor", None),
        P("serve", None, "tensor", None),
        P("serve", None, "tensor", None),
        P("serve"),
        P("serve"),
        P("serve"),
    )
    return jax.shard_map(
        shards, mesh=mesh, in_specs=placed, out_specs=P(("serve", "tensor"), None), check_vma=False
    )
```

time: 266 us -> 119 us (0.45)
  blocking collectives: 147 us -> 99.6 us
  waiting for transfers between devices: 43.1 us -> 0 us
  other arithmetic: 21.5 us -> 0 us
  starting transfers between devices: 19.5 us -> 0 us
  local copies, waits for them, and re-layouts: 22.5 us -> 8.15 us
  Pallas kernels: 0 us -> 10.5 us
  matrix products: 9.61 us -> 0 us
    all_to_all x0 -> x2, blocking collectives: none -> 86.3 us  [the longest x1 49.3 us: shards(): lax.all_to_all(message, 'serve', split_axis=0, concat_axis=0, tiled=True)]
    all_gather x1 -> x0, blocking collectives: 81.3 us -> none  [shards(): far_rows = lax.all_gather(long_rows, 'serve', axis=0, tiled=True)]
    all_to_all x3 -> x0, waiting for transfers between devices: 43.1 us -> none  [the longest x1 19 us: shards(): lax.all_to_all(remote_out, 'serve', split_axis=0, concat_axis=0, tiled=True)]
    all_to_all x1, blocking collectives: 45.6 us -> 13.3 us  [shards(): lax.all_to_all(rows_out, 'tensor', split_axis=0, concat_axis=1, tiled=True)]
    unnamed x1 -> x0, blocking collectives: 19.8 us -> none
    all_to_all x3 -> x0, starting transfers between devices: 19.5 us -> none  [the longest x1 9.4 us: shards(): lax.all_to_all(remote_sum, 'serve', split_axis=0, concat_axis=0, tiled=True)]
    pallas_call x0 -> x3, Pallas kernels: none -> 10.5 us  [the longest x1 6.58 us: shards(): pl.pallas_call(functools.partial(main_kernel, chunk, scale2), out_shape=(...]
    dot_general x6 -> x0, matrix products: 9.61 us -> none  [the longest x2 4.02 us: block_partial(): jnp.einsum('bkgst,btkh->bkgsh', weights, values, preferred_element_type=j...]
  transfers between devices with their start and end apart: 3 -> 0, of which waited for: 3 -> 0; matrix products, arithmetic and copies ran while one was open for 7% -> 0% of each run, Pallas kernels for 0% -> 0%
where the time goes in v1:
time: 119 us; the launch traced here: 118 us
  blocking collectives  99.6 us (84%)
  Pallas kernels  10.5 us (9%)
  local copies, waits for them, and re-layouts  8.15 us (7%)
    all_to_all x1, blocking collectives, shards(): lax.all_to_all(message, 'serve', split_axis=0, concat_axis=0, tiled=True)  49.3 us
    all_to_all x1, blocking collectives, shards(): got = lax.all_to_all(back, 'serve', split_axis=0, concat_axis=0, tiled=True)  37 us
    all_to_all x1, blocking collectives, shards(): lax.all_to_all(rows_out, 'tensor', split_axis=0, concat_axis=1, tiled=True)  13.3 us
    unnamed x19, local copies, waits for them, and re-layouts  7.39 us
    pallas_call x1, Pallas kernels, shards(): pl.pallas_call(functools.partial(main_kernel, chunk, scale2), out_shape=(...  6.58 us

profile of v1, /device:TPU:1, one launch (start us, length us, event | category | flops | bytes accessed | tf_op | source)
XLA Modules:
  0.0 118.3 jit_solution(8005582154769574015)
XLA Ops:
  0.0 1.6 %prep.1 = (bf16[4,32,128]{2,1,0:T(8,128)(2,1)}, bf16[64,32,128]{2,1,0:T(8,128)(2,1)}) custom-call(s32[4]{0:T(128)} %lengths.3, bf16[4,7,4,128]{3,2,1,0:T(4,128)(2,1)} %bitcast.13), custom_call_target="tpu_custom_call" | custom-call | tf_op jit(solution)/shard_map/prep/pallas_call | solution.py:215
  1.6 49.3 %all_to_all.29.far = bf16[64,32,128]{2,1,0:T(8,128)(2,1)S(1)} all-to-all(bf16[64,32,128]{2,1,0:T(8,128)(2,1)} %get-tuple-element.10), channel_id=1, replica_groups=mesh['serve'=64,'tensor'=8] {'serve'}, dimensions={0} | all-to-all | bytes 1048576 | tf_op jit(solution)/shard_map/all_to_all | solution.py:226
  50.9 0.0 copy-start
  50.9 1.7 %copy-done = bf16[36,256,1,128]{3,1,2,0:T(8,128)(2,1)S(1)} copy-done((bf16[36,256,1,128]{3,1,2,0:T(8,128)(2,1)S(1)}, bf16[36,256,1,128]{3,1,2,0:T(8,128)(2,1)}, u32[]{:S(2)}) %copy-start) | copy-done | bytes 2359320
  52.6 0.0 copy-start.1
  52.6 1.7 %copy-done.1 = bf16[36,256,1,128]{3,1,2,0:T(8,128)(2,1)S(1)} copy-done((bf16[36,256,1,128]{3,1,2,0:T(8,128)(2,1)S(1)}, bf16[36,256,1,128]{3,1,2,0:T(8,128)(2,1)}, u32[]{:S(2)}) %copy-start.1) | copy-done | bytes 2359320
  54.2 0.0 copy-start.4
  54.2 0.8 copy-done.4
  55.0 0.0 copy-start.5
  55.0 0.7 copy-done.5
  55.7 0.0 copy-start.6
  55.7 0.7 copy-done.6
  56.4 0.0 copy-start.7
  56.4 0.7 copy-done.7
  57.0 0.0 copy-start.8
  57.0 0.7 copy-done.8
  57.7 6.6 %blocks.1 = (bf16[64,32,128]{2,1,0:T(8,128)(2,1)S(1)}, f32[4,32,128]{2,1,0:T(8,128)S(1)}, f32[4,32,128]{2,1,0:T(8,128)S(1)}) custom-call(s32[36]{0:T(128)S(1)} %copy-done.7, s32[36]{0:T(128)S(1)} %copy-done.8, bf16[64,32,128]{2,1,0:T(8,128)(2,1)S(1)} %all_to_all.29.far, bf16[4,32,128]{2,1,0:T(8,128)(2,1)S(1)} %copy-done.4, bf16[4,4,128]{2,1,0:T(4,128)(2,1)S(1)} %bitcast.10, ...), custom_call_target="tpu_custom_call" | custom-call | tf_op jit(solution)/shard_map/blocks/pallas_call | solution.py:227
  64.3 0.0 copy-start.2
  64.3 0.0 copy-start.3
  64.3 37.0 %all_to_all.30.got = bf16[64,32,128]{2,1,0:T(8,128)(2,1)} all-to-all(bf16[64,32,128]{2,1,0:T(8,128)(2,1)S(1)} %get-tuple-element.12), channel_id=1, replica_groups=mesh['serve'=64,'tensor'=8] {'serve'}, dimensions={0} | all-to-all | bytes 1048576 | tf_op jit(solution)/shard_map/all_to_all | solution.py:246
  101.3 0.0 copy-done.2
  101.3 0.0 copy-done.3
  101.3 2.3 %combine.1 = bf16[16,896]{1,0:T(8,128)(2,1)} custom-call(s32[4]{0:T(128)} %lengths.3, bf16[64,32,128]{2,1,0:T(8,128)(2,1)} %all_to_all.30.got, f32[4,32,128]{2,1,0:T(8,128)} %copy-done.2, f32[4,32,128]{2,1,0:T(8,128)} %copy-done.3), custom_call_target="tpu_custom_call" | custom-call | tf_op jit(solution)/shard_map/combine/pallas_call | solution.py:247
  103.6 0.8 all_to_all.22
  104.4 13.3 %all_to_all.31 = bf16[8,2,896]{2,1,0:T(2,128)(2,1)S(1)} all-to-all(bf16[8,2,896]{2,1,0:T(2,128)(2,1)S(1)} %all_to_all.22), channel_id=1, replica_groups=mesh['serve'=64,'tensor'=8] {'tensor'}, dimensions={0} | all-to-all | bytes 57344 | tf_op jit(solution)/shard_map/all_to_all | solution.py:254
  117.7 0.6 copy.11
Async XLA Ops:
  50.9 1.7 %copy-start = (bf16[36,256,1,128]{3,1,2,0:T(8,128)(2,1)S(1)}, bf16[36,256,1,128]{3,1,2,0:T(8,128)(2,1)}, u32[]{:S(2)}) copy-start(bf16[36,256,1,128]{3,1,2,0:T(8,128)(2,1)} %param.11) | copy-start | bytes 7077892
  52.6 1.7 %copy-start.1 = (bf16[36,256,1,128]{3,1,2,0:T(8,128)(2,1)S(1)}, bf16[36,256,1,128]{3,1,2,0:T(8,128)(2,1)}, u32[]{:S(2)}) copy-start(bf16[36,256,1,128]{3,1,2,0:T(8,128)(2,1)} %param.12) | copy-start | bytes 7077892
  54.2 0.8 copy-start.4
  55.0 0.7 copy-start.5
  55.7 0.7 copy-start.6
  56.4 0.7 copy-start.7
  57.0 0.7 copy-start.8
  64.3 37.1 %copy-start.2 = (f32[4,32,128]{2,1,0:T(8,128)}, f32[4,32,128]{2,1,0:T(8,128)S(1)}, u32[]{:S(2)}) copy-start(f32[4,32,128]{2,1,0:T(8,128)S(1)} %get-tuple-element.13.local_out) | copy-start | bytes 196612
  64.3 37.0 %copy-start.3 = (f32[4,32,128]{2,1,0:T(8,128)}, f32[4,32,128]{2,1,0:T(8,128)S(1)}, u32[]{:S(2)}) copy-start(f32[4,32,128]{2,1,0:T(8,128)S(1)} %get-tuple-element.14.local_lse) | copy-start | bytes 196612

commit v2 on v1

--- a/solution.py
+++ b/solution.py
@@ -16,6 +16,24 @@
 
 def iota(shape, dim):
     return lax.broadcasted_iota(jnp.int32, shape, dim)
+
+
+def column_first(device):
+    return lax.bitwise_and(device, 3) * 16 + lax.shift_right_logical(device, 2)
+
+
+def message_of(out, lse, rows):
+    row = iota(out.shape, 0)
+    high = lse.astype(BF16).astype(F32)
+    rest = lse - high
+    middle = rest.astype(BF16).astype(F32)
+    low = rest - middle
+    stats = jnp.where(
+        row == rows,
+        high,
+        jnp.where(row == rows + 1, middle, jnp.where(row == rows + 2, low, 0.0)),
+    )
+    return jnp.where(row < rows, out, stats).astype(BF16)
 
 
 def prep_kernel(lengths, queries, own, message, padded):
@@ -89,10 +107,11 @@
         owner = [owners[p] for p in ids]
         device = [lax.shift_right_logical(o, 2) for o in owner]
         mine = [d == me for d in device]
+        place = [column_first(d) for d in device]
         raw = []
         for k, p in enumerate(ids):
             slot = lax.bitwise_and(owner[k], 3)
-            query = jnp.where(mine[k], own[slot], far[device[k]])
+            query = jnp.where(mine[k], own[slot], far[place[k]])
             lens = query[rows : rows + 2, :].astype(F32)
             length = lens[0:1, 0:1] * 64.0 + lens[1:2, 0:1]
             score = lax.dot_general(
@@ -116,17 +135,8 @@
             block_out[p] = out
             block_lse[p] = column
             flat = jnp.sum(jnp.where(diagonal, column, 0.0), axis=0, keepdims=True)
-            high = flat.astype(BF16).astype(F32)
-            rest = flat - high
-            middle = rest.astype(BF16).astype(F32)
-            low = rest - middle
-            stats = jnp.where(
-                row == rows,
-                high,
-                jnp.where(row == rows + 1, middle, jnp.where(row == rows + 2, low, 0.0)),
-            )
-            back[device[k]] = jnp.where(row < rows, out, stats).astype(BF16)
-    back[me] = empty
+            back[place[k]] = message_of(out, flat, rows)
+    back[column_first(me)] = empty
 
     def merge(p, carry):
         owner = owners[p]
@@ -144,6 +154,44 @@
         return carry
 
     lax.fori_loop(0, blocks, merge, 0)
+
+
+def four_fold(x, op):
+    x = op(x, pltpu.roll(x, 2 * PAD, 1))
+    return op(x, pltpu.roll(x, PAD, 1))
+
+
+def stage_kernel(got, onward):
+    sources, many, _, head_dim = got.shape
+    rows = 28
+    me = lax.axis_index("serve")
+    depth = sources * many * PAD
+    flat = got[...].reshape(depth, head_dim)
+    g2, k2 = iota((many, depth), 0), iota((many, depth), 1)
+    in_row = jnp.logical_and(k2 % PAD >= rows, k2 % PAD < rows + 3)
+    pick = jnp.logical_and((k2 // PAD) % many == g2, in_row)
+    lse = lax.dot_general(
+        jnp.where(pick, 1.0, 0.0).astype(BF16), flat, (((1,), (0,)), ((), ())),
+        preferred_element_type=F32,
+    )
+    top = four_fold(lse, jnp.maximum)
+    weight = jnp.exp2(lse - top)
+    total = four_fold(weight, jnp.add)
+    weight = weight / total
+    row, lane = iota((PAD, head_dim), 0), iota((PAD, head_dim), 1)
+    same = jnp.logical_and(lane % PAD == row, row < rows)
+    offset = lax.bitwise_and(lax.shift_right_logical(me, 2), 3) * PAD
+    lane = iota((many, head_dim), 1)
+    in_span = jnp.logical_and(lane >= offset, lane < offset + rows)
+    lse = jnp.where(in_span, top + jnp.log2(total), 0.0)
+    for m in range(many):
+        spread = jnp.where(same, weight[m : m + 1], 0.0)
+        high = spread.astype(BF16)
+        low = (spread - high.astype(F32)).astype(BF16)
+        both = jnp.concatenate([high, low], axis=0)
+        block = got[:, m].reshape(sources * PAD, head_dim)
+        out = lax.dot_general(both, block, (((1,), (0,)), ((), ())), preferred_element_type=F32)
+        onward[m] = message_of(out[:PAD] + out[PAD:], lse[m : m + 1], rows)
 
 
 def combine_kernel(lengths, got, local_out, local_lse, result):
@@ -162,8 +210,7 @@
     )
     top = jnp.max(lse, axis=0, keepdims=True)
     top = jnp.broadcast_to(top, (8, head_dim))
-    top = jnp.maximum(top, pltpu.roll(top, 2 * PAD, 1))
-    top = jnp.maximum(top, pltpu.roll(top, PAD, 1))
+    top = four_fold(top, jnp.maximum)
     weight = jnp.exp2(lse - top[0:1])
     row, lane = iota((PAD, head_dim), 0), iota((PAD, head_dim), 1)
     same = jnp.logical_and(lane % PAD == row, row < rows)
@@ -188,14 +235,15 @@
         a, b = jnp.exp2(far_here - overall), jnp.exp2(near - overall)
         final = ((a * far_out + b * local_out[slot]) / (a + b)).astype(BF16)
         for g in range(groups):
-            result[slot * steps : (slot + 1) * steps, g * head_dim : (g + 1) * head_dim] = final[
-                g * steps : (g + 1) * steps
-            ]
+            columns = slice(g * head_dim, (g + 1) * head_dim)
+            for half in range(2):
+                start = g * steps + half * 2
+                result[slot * 2 + half, :, columns] = final[start : start + 2]
 
 
 VMEM = pl.BlockSpec(memory_space=pltpu.VMEM)
 SMEM = pl.BlockSpec(memory_space=pltpu.SMEM)
-ANY = pl.BlockSpec(memory_space=pl.ANY)
+HBM = pl.BlockSpec(memory_space=pltpu.HBM)
 
 
 def shards(
@@ -212,18 +260,24 @@
     key_cache = key_cache.reshape(blocks, span, head_dim)
     value_cache = value_cache.reshape(blocks, span, head_dim)
 
+    along_z = [[4 * z + y for z in range(16)] for y in range(4)]
+    along_y = [[4 * z + y for y in range(4)] for z in range(16)]
+    exchange = functools.partial(
+        lax.all_to_all, axis_name="serve", split_axis=0, concat_axis=0, tiled=True
+    )
     own, message = pl.pallas_call(
         prep_kernel,
         out_shape=(
             jax.ShapeDtypeStruct((slots, PAD, head_dim), BF16),
-            jax.ShapeDtypeStruct((devices, PAD, head_dim), BF16),
+            jax.ShapeDtypeStruct((16, PAD, head_dim), BF16),
         ),
         in_specs=[SMEM, VMEM],
         out_specs=(VMEM, VMEM),
         scratch_shapes=[pltpu.VMEM((slots, PAD, head_dim), F32)],
         name="prep",
     )(lengths, queries)
-    far = lax.all_to_all(message, "serve", split_axis=0, concat_axis=0, tiled=True)
+    column = exchange(message, axis_index_groups=along_z)
+    far = exchange(jnp.broadcast_to(column[None], (4,) + column.shape), axis_index_groups=along_y)
     back, local_out, local_lse = pl.pallas_call(
         functools.partial(main_kernel, chunk, scale2),
         out_shape=(
@@ -231,7 +285,7 @@
             jax.ShapeDtypeStruct((slots, PAD, head_dim), F32),
             jax.ShapeDtypeStruct((slots, PAD, head_dim), F32),
         ),
-        in_specs=[SMEM, SMEM, VMEM, VMEM, VMEM, VMEM, ANY, ANY],
+        in_specs=[SMEM, SMEM, VMEM, VMEM, VMEM, VMEM, HBM, HBM],
         out_specs=(VMEM, VMEM, VMEM),
         scratch_shapes=[
             pltpu.VMEM((blocks, span, head_dim), BF16),
@@ -240,18 +294,31 @@
             pltpu.VMEM((blocks, PAD, head_dim), F32),
             pltpu.SemaphoreType.DMA((2, blocks // chunk)),
         ],
-        compiler_params=pltpu.CompilerParams(vmem_limit_bytes=24 << 20),
+        compiler_params=pltpu.CompilerParams(vmem_limit_bytes=56 << 20),
         name="blocks",
-    )(block_owner, block_number, far, own, new_keys, new_values, key_cache, value_cache)
-    got = lax.all_to_all(back, "serve", split_axis=0, concat_axis=0, tiled=True)
+    )(
+        block_owner, block_number, far.reshape(devices, PAD, head_dim), own,
+        new_keys, new_values, key_cache, value_cache,
+    )
+    back = back.reshape(4, 16, PAD, head_dim)
+    row_got = exchange(back, axis_index_groups=along_y)
+    onward = pl.pallas_call(
+        stage_kernel,
+        out_shape=jax.ShapeDtypeStruct((16, PAD, head_dim), BF16),
+        in_specs=[VMEM],
+        out_specs=VMEM,
+        name="stage",
+    )(row_got)
+    got = exchange(onward, axis_index_groups=along_z)
     rows_out = pl.pallas_call(
         combine_kernel,
-        out_shape=jax.ShapeDtypeStruct((slots * steps, groups * head_dim), BF16),
+        out_shape=jax.ShapeDtypeStruct((8, 2, groups * head_dim), BF16),
         in_specs=[SMEM, VMEM, VMEM, VMEM],
         out_specs=VMEM,
         name="combine",
     )(lengths, got, local_out, local_lse)
-    return lax.all_to_all(rows_out, "tensor", split_axis=0, concat_axis=1, tiled=True)
+    swapped = lax.all_to_all(rows_out, "tensor", split_axis=0, concat_axis=0, tiled=True)
+    return jnp.transpose(swapped, (1, 0, 2)).reshape(2, 8 * groups * head_dim)
 
 
 def solution(mesh):

time: 119 us -> 96.7 us (0.81)
  blocking collectives: 99.6 us -> 83 us
  local copies, waits for them, and re-layouts: 8.15 us -> 0.68 us
  Pallas kernels: 10.5 us -> 12.4 us
    all_to_all x3 -> x5, blocking collectives: 99.6 us -> 83 us  [the longest x1 27.7 us: shards(): column = exchange(message, axis_index_groups=along_z)]
    unnamed x19 -> x1, local copies, waits for them, and re-layouts: 7.39 us -> 0.61 us
    pallas_call x1 -> x2, Pallas kernels: 2.26 us -> 4.43 us  [the longest x1 2.42 us: shards(): pl.pallas_call(stage_kernel, out_shape=jax.ShapeDtypeStruct((16, PAD, hea...]
where the time goes in v2:
time: 96.7 us; the launch traced here: 96.1 us
  blocking collectives  83 us (86%)
  Pallas kernels  12.4 us (13%)
    all_to_all x1, blocking collectives, shards(): column = exchange(message, axis_index_groups=along_z)  27.7 us
    all_to_all x1, blocking collectives, shards(): got = exchange(onward, axis_index_groups=along_z)  19 us
    all_to_all x1, blocking collectives, shards(): lax.all_to_all(rows_out, 'tensor', split_axis=0, concat_axis=0, tiled=True)  14.1 us
    all_to_all x1, blocking collectives, shards(): row_got = exchange(back, axis_index_groups=along_y)  11.1 us
    all_to_all x1, blocking collectives, shards(): exchange(jnp.broadcast_to(column[None], (4,) + column.shape), axis_index_...  11 us
    pallas_call x1, Pallas kernels, shards(): pl.pallas_call(functools.partial(main_kernel, chunk, scale2), out_shape=(...  6.52 us
    pallas_call x1, Pallas kernels, shards(): pl.pallas_call(stage_kernel, out_shape=jax.ShapeDtypeStruct((16, PAD, hea...  2.42 us
    pallas_call x1, Pallas kernels, shards(): pl.pallas_call(combine_kernel, out_shape=jax.ShapeDtypeStruct((8, 2, grou...  2.01 us

profile of v2, /device:TPU:1, one launch (start us, length us, event | category | flops | bytes accessed | tf_op | source)
XLA Modules:
  0.0 96.1 jit_solution(2958996084180980806)
XLA Ops:
  0.0 1.4 %prep.1 = (bf16[4,32,128]{2,1,0:T(8,128)(2,1)}, bf16[16,32,128]{2,1,0:T(8,128)(2,1)}) custom-call(s32[4]{0:T(128)} %lengths.3, bf16[4,7,4,128]{3,2,1,0:T(4,128)(2,1)} %bitcast.15), custom_call_target="tpu_custom_call" | custom-call | tf_op jit(solution)/shard_map/prep/pallas_call | solution.py:268
  1.4 27.7 %all_to_all.25 = bf16[16,32,128]{2,1,0:T(8,128)(2,1)S(1)} all-to-all(bf16[16,32,128]{2,1,0:T(8,128)(2,1)} %get-tuple-element.10), channel_id=1, replica_groups={{0,32,64,96,128,160,192,224,256,288,320,352,384,416,448,480},{8,40,72,1..., dimensions={0} | all-to-all | bytes 262144 | tf_op jit(solution)/shard_map/all_to_all | solution.py:279
  29.2 0.1 broadcast_in_dim.2
  29.3 11.0 %all_to_all.26 = bf16[4,16,32,128]{3,2,1,0:T(8,128)(2,1)} all-to-all(bf16[4,16,32,128]{3,2,1,0:T(8,128)(2,1)S(1)} %broadcast_in_dim.2), channel_id=1, replica_groups={{0,8,16,24},{32,40,48,56},{64,72,80,88},{96,104,112,120},{128,136,144,1..., dimensions={0} | all-to-all | bytes 1048576 | tf_op jit(solution)/shard_map/all_to_all | solution.py:280
  40.3 6.5 %blocks.1 = (bf16[64,32,128]{2,1,0:T(8,128)(2,1)}, f32[4,32,128]{2,1,0:T(8,128)}, f32[4,32,128]{2,1,0:T(8,128)}) custom-call(s32[36]{0:T(128)} %owners.1, s32[36]{0:T(128)} %numbers.1, bf16[64,32,128]{2,1,0:T(8,128)(2,1)} %bitcast.12, bf16[4,32,128]{2,1,0:T(8,128)(2,1)} %get-tuple-element.11.own, bf16[4,4,128]{2,1,0:T(4,128)(2,1)} %bitcast.16, ...), custom_call_target="tpu_custom_call" | custom-call | tf_op jit(solution)/shard_map/blocks/pallas_call | solution.py:281
  46.8 11.1 %all_to_all.27.got = bf16[4,16,32,128]{3,2,1,0:T(8,128)(2,1)} all-to-all(bf16[4,16,32,128]{3,2,1,0:T(8,128)(2,1)} %bitcast.13), channel_id=1, replica_groups={{0,8,16,24},{32,40,48,56},{64,72,80,88},{96,104,112,120},{128,136,144,1..., dimensions={0} | all-to-all | bytes 1048576 | tf_op jit(solution)/shard_map/all_to_all | solution.py:304
  58.0 2.4 %stage.1 = bf16[16,32,128]{2,1,0:T(8,128)(2,1)} custom-call(bf16[4,16,32,128]{3,2,1,0:T(8,128)(2,1)} %all_to_all.27.got), custom_call_target="tpu_custom_call" | custom-call | tf_op jit(solution)/shard_map/stage/pallas_call | solution.py:305
  60.4 19.0 %all_to_all.28.got = bf16[16,32,128]{2,1,0:T(8,128)(2,1)} all-to-all(bf16[16,32,128]{2,1,0:T(8,128)(2,1)} %stage.1), channel_id=1, replica_groups={{0,32,64,96,128,160,192,224,256,288,320,352,384,416,448,480},{8,40,72,1..., dimensions={0} | all-to-all | bytes 262144 | tf_op jit(solution)/shard_map/all_to_all | solution.py:312
  79.4 2.0 %combine.1 = bf16[8,2,896]{2,1,0:T(2,128)(2,1)} custom-call(s32[4]{0:T(128)} %lengths.3, bf16[16,32,128]{2,1,0:T(8,128)(2,1)} %all_to_all.28.got, f32[4,32,128]{2,1,0:T(8,128)} %get-tuple-element.13.local_out, f32[4,32,128]{2,1,0:T(8,128)} %get-tuple-element.14.local_lse), custom_call_target="tpu_custom_call" | custom-call | tf_op jit(solution)/shard_map/combine/pallas_call | solution.py:313
  81.4 14.1 %all_to_all.29 = bf16[8,2,896]{2,1,0:T(2,128)(2,1)S(1)} all-to-all(bf16[8,2,896]{2,1,0:T(2,128)(2,1)} %combine.1), channel_id=1, replica_groups=mesh['serve'=64,'tensor'=8] {'tensor'}, dimensions={0} | all-to-all | bytes 57344 | tf_op jit(solution)/shard_map/all_to_all | solution.py:320
  95.5 0.6 copy.10

commit v3 on v2

v3 whole, which is shorter than its diff:
```python
import functools
import math

import jax
import jax.numpy as jnp
from jax import lax
from jax.experimental import pallas as pl
from jax.experimental.pallas import tpu as pltpu
from jax.sharding import PartitionSpec as P

neg_fill = -1e30
PAD = 32
F32 = jnp.float32
BF16 = jnp.bfloat16


def iota(shape, dim):
    return lax.broadcasted_iota(jnp.int32, shape, dim)


def column_first(device):
    return lax.bitwise_and(device, 3) * 16 + lax.shift_right_logical(device, 2)


def message_of(out, lse, rows):
    row = iota(out.shape, 0)
    high = lse.astype(BF16).astype(F32)
    rest = lse - high
    middle = rest.astype(BF16).astype(F32)
    low = rest - middle
    stats = jnp.where(
        row == rows,
        high,
        jnp.where(row == rows + 1, middle, jnp.where(row == rows + 2, low, 0.0)),
    )
    return jnp.where(row < rows, out, stats).astype(BF16)


def pad_rows(length, query, padded):
    groups, steps, head_dim = query.shape
    rows = groups * steps
    for g in range(groups):
        padded[g * steps : (g + 1) * steps, :] = query[g].astype(F32)
    row = iota((PAD - rows, head_dim), 0)
    high = lax.shift_right_logical(length, 6).astype(F32)
    low = lax.bitwise_and(length, 63).astype(F32)
    padded[rows:PAD, :] = jnp.where(row == 0, high, jnp.where(row == 1, low, 0.0))


def fetch(pairs, sems):
    copies = [
        pltpu.make_async_copy(source, target, sems.at[i])
        for i, (source, target) in enumerate(pairs)
    ]
    for copy in copies:
        copy.start()
    return copies


def prep_kernel(lengths_hbm, queries_hbm, message, lengths, queries, padded, sems):
    copies = fetch(((lengths_hbm, lengths), (queries_hbm, queries)), sems)
    for copy in copies:
        copy.wait()
    long_slot, length = jnp.int32(0), lengths[0]
    for slot in range(1, queries.shape[0]):
        is_long = lengths[slot] > 256
        long_slot = jnp.where(is_long, slot, long_slot)
        length = jnp.where(is_long, lengths[slot], length)
    pad_rows(length, queries.at[long_slot], padded)
    message[...] = jnp.broadcast_to(padded[...].astype(BF16)[None], message.shape)


def attend(query, limit, keys, values, scale2):
    score = lax.dot_general(query, keys, (((1,), (1,)), ((), ())), preferred_element_type=F32)
    score = jnp.where(iota(score.shape, 1).astype(F32) < limit, score, neg_fill)
    top = jnp.max(score, axis=1, keepdims=True)
    weights = jnp.exp2((score - top) * scale2).astype(BF16)
    total = jnp.sum(weights.astype(F32), axis=1, keepdims=True)
    out = lax.dot_general(weights, values, (((1,), (0,)), ((), ())), preferred_element_type=F32)
    return out / total, top * scale2 + jnp.log2(total)


def local_kernel(
    scale2, lengths_hbm, owners_hbm, numbers_hbm, queries_hbm, new_keys_hbm, new_values_hbm,
    key_cache, value_cache,
    keys, table, local_out, local_lse,
    lengths, owners, numbers, queries, new_keys, new_values, padded, one_value, sems,
):
    blocks, span, head_dim = keys.shape
    slots, steps, _ = new_keys.shape
    me = lax.axis_index("serve")
    small = ((lengths_hbm, lengths), (owners_hbm, owners), (numbers_hbm, numbers),
             (queries_hbm, queries), (new_keys_hbm, new_keys), (new_values_hbm, new_values))
    copies = fetch(small + ((key_cache, keys),), sems)
    for copy in copies[: len(small)]:
        copy.wait()

    def place(p, counts):
        far_count, near_count = counts
        device = lax.shift_right_logical(owners[p], 2)
        near = device == me
        at = jnp.where(near, blocks - 1 - near_count, far_count)
        table[at] = p
        table[64 + at] = jnp.where(near, lax.bitwise_and(owners[p], 3), column_first(device))
        table[128 + at] = numbers[p] * span
        one = near.astype(jnp.int32)
        return far_count + 1 - one, near_count + one

    far_count, near_count = lax.fori_loop(0, blocks, place, (jnp.int32(0), jnp.int32(0)))
    table[192] = far_count

    for slot in range(slots):
        pad_rows(lengths[slot], queries.at[slot], padded.at[slot])
    all_rows = padded[...].astype(BF16).reshape(slots * PAD, head_dim)
    nk = new_keys[...].astype(F32).reshape(slots * steps, head_dim).astype(BF16)
    nv = new_values[...].astype(F32).reshape(slots * steps, head_dim).astype(BF16)
    scores = lax.dot_general(all_rows, nk, (((1,), (1,)), ((), ())), preferred_element_type=F32)
    r2, c2 = iota(scores.shape, 0), iota(scores.shape, 1)
    seen = jnp.logical_and(r2 // PAD == c2 // steps, c2 % steps <= r2 % steps)
    scores = jnp.where(seen, scores, neg_fill)
    top = jnp.max(scores, axis=1, keepdims=True)
    weights = jnp.where(seen, jnp.exp2((scores - top) * scale2), 0.0).astype(BF16)
    total = jnp.sum(weights.astype(F32), axis=1, keepdims=True)
    out = lax.dot_general(weights, nv, (((1,), (0,)), ((), ())), preferred_element_type=F32)
    lse = jnp.broadcast_to(top * scale2 + jnp.log2(total), out.shape)
    local_out[...] = (out / total).reshape(local_out.shape)
    local_lse[...] = lse.reshape(local_lse.shape)
    for copy in copies[len(small) :]:
        copy.wait()

    def merge(k, carry):
        p, slot = table[blocks - 1 - k], table[64 + blocks - 1 - k]
        copy = pltpu.make_async_copy(value_cache.at[p], one_value, sems.at[7])
        copy.start()
        copy.wait()
        limit = (lengths[slot] - table[128 + blocks - 1 - k]).astype(F32)
        new_out, new = attend(padded[slot].astype(BF16), limit, keys[p], one_value[...], scale2)
        old, new = local_lse[slot], jnp.broadcast_to(new, new_out.shape)
        overall = jnp.maximum(old, new)
        a, b = jnp.exp2(old - overall), jnp.exp2(new - overall)
        total = a + b
        local_out[slot] = (a * local_out[slot] + b * new_out) / total
        local_lse[slot] = overall + jnp.log2(total)
        return carry

    lax.fori_loop(0, near_count, merge, 0)


def far_kernel(chunk, scale2, table, far, keys, value_cache, back, values, sems):
    blocks, span, head_dim = keys.shape
    rows = 28
    count = blocks - 4
    me = lax.axis_index("serve")
    far_count = table[192]
    copies = fetch([(value_cache.at[table[k]], values.at[k]) for k in range(count)], sems)
    row, lane = iota((PAD, head_dim), 0), iota((PAD, head_dim), 1)
    offset = lax.bitwise_and(me, 3) * PAD
    diagonal = jnp.logical_and(lane == offset + row, row < rows)
    in_span = jnp.logical_and(lane >= offset, lane < offset + rows)
    empty = jnp.where(jnp.logical_and(row == rows, in_span), neg_fill, 0.0).astype(BF16)
    back[...] = jnp.broadcast_to(empty[None], back.shape)
    unused = column_first(me)
    position = iota((PAD, span), 1).astype(F32)
    for c in range(count // chunk):
        ids = [table[k] for k in range(c * chunk, (c + 1) * chunk)]
        places = [
            jnp.where(k < far_count, table[64 + k], unused)
            for k in range(c * chunk, (c + 1) * chunk)
        ]
        raw = []
        for k in range(chunk):
            query = far[places[k]]
            lens = query[rows : rows + 2, :].astype(F32)
            length = lens[0:1, 0:1] * 64.0 + lens[1:2, 0:1]
            score = lax.dot_general(
                query, keys[ids[k]], (((1,), (1,)), ((), ())), preferred_element_type=F32
            )
            limit = length - table[128 + c * chunk + k].astype(F32)
            raw.append(jnp.where(position < limit, score, neg_fill))
        raw = jnp.concatenate(raw, axis=0)
        top = jnp.max(raw, axis=1, keepdims=True)
        weights = jnp.exp2((raw - top) * scale2).astype(BF16)
        total = jnp.sum(weights.astype(F32), axis=1, keepdims=True)
        lse = top * scale2 + jnp.log2(total)
        inverse = 1.0 / total
        for k in range(chunk):
            part = slice(k * PAD, (k + 1) * PAD)
            copies[c * chunk + k].wait()
            out = lax.dot_general(
                weights[part], values[c * chunk + k], (((1,), (0,)), ((), ())),
                preferred_element_type=F32,
            )
            flat = jnp.sum(jnp.where(diagonal, lse[part], 0.0), axis=0, keepdims=True)
            back[places[k]] = message_of(out * inverse[part], flat, rows)
    back[unused] = empty


def four_fold(x, op):
    x = op(x, pltpu.roll(x, 2 * PAD, 1))
    return op(x, pltpu.roll(x, PAD, 1))


def stage_kernel(got, onward):
    sources, many, _, head_dim = got.shape
    rows = 28
    me = lax.axis_index("serve")
    depth = sources * many * PAD
    flat = got[...].reshape(depth, head_dim)
    g2, k2 = iota((many, depth), 0), iota((many, depth), 1)
    in_row = jnp.logical_and(k2 % PAD >= rows, k2 % PAD < rows + 3)
    pick = jnp.logical_and((k2 // PAD) % many == g2, in_row)
    lse = lax.dot_general(
        jnp.where(pick, 1.0, 0.0).astype(BF16), flat, (((1,), (0,)), ((), ())),
        preferred_element_type=F32,
    )
    top = four_fold(lse, jnp.maximum)
    weight = jnp.exp2(lse - top)
    total = four_fold(weight, jnp.add)
    weight = weight / total
    row, lane = iota((PAD, head_dim), 0), iota((PAD, head_dim), 1)
    same = jnp.logical_and(lane % PAD == row, row < rows)
    offset = lax.bitwise_and(lax.shift_right_logical(me, 2), 3) * PAD
    lane = iota((many, head_dim), 1)
    in_span = jnp.logical_and(lane >= offset, lane < offset + rows)
    lse = jnp.where(in_span, top + jnp.log2(total), 0.0)
    for m in range(many):
        spread = jnp.where(same, weight[m : m + 1], 0.0)
        high = spread.astype(BF16)
        low = (spread - high.astype(F32)).astype(BF16)
        both = jnp.concatenate([high, low], axis=0)
        block = got[:, m].reshape(sources * PAD, head_dim)
        out = lax.dot_general(both, block, (((1,), (0,)), ((), ())), preferred_element_type=F32)
        onward[m] = message_of(out[:PAD] + out[PAD:], lse[m : m + 1], rows)


def combine_kernel(lengths_hbm, got, local_out, local_lse, result, lengths, sems):
    copies = fetch(((lengths_hbm, lengths),), sems)
    devices, _, head_dim = got.shape
    slots = local_out.shape[0]
    steps, groups, rows = 4, 7, 28
    depth = devices * PAD
    many = devices // 4
    flat = got[...].reshape(depth, head_dim)
    g2, k2 = iota((many, depth), 0), iota((many, depth), 1)
    in_row = jnp.logical_and(k2 % PAD >= rows, k2 % PAD < rows + 3)
    pick = jnp.logical_and(k2 // (4 * PAD) == g2, in_row)
    lse = lax.dot_general(
        jnp.where(pick, 1.0, 0.0).astype(BF16), flat, (((1,), (0,)), ((), ())),
        preferred_element_type=F32,
    )
    top = jnp.max(lse, axis=0, keepdims=True)
    top = jnp.broadcast_to(top, (8, head_dim))
    top = four_fold(top, jnp.maximum)
    weight = jnp.exp2(lse - top[0:1])
    row, lane = iota((PAD, head_dim), 0), iota((PAD, head_dim), 1)
    same = jnp.logical_and(lane % PAD == row, row < rows)
    spread = jnp.concatenate(
        [jnp.where(same, weight[g : g + 1], 0.0) for g in range(many)], axis=1
    )
    high = spread.astype(BF16)
    low = (spread - high.astype(F32)).astype(BF16)
    both = jnp.concatenate([high, low], axis=0)
    out = lax.dot_general(both, flat, (((1,), (0,)), ((), ())), preferred_element_type=F32)
    out = out[:PAD] + out[PAD:]
    total = jnp.sum(spread, axis=1, keepdims=True)
    total = jnp.where(row[:, 0:1] < rows, total, 1.0)
    first = jnp.logical_and(lane == row, row < rows)
    column = jnp.sum(jnp.where(first, top[0:1], 0.0), axis=1, keepdims=True)
    far_out = out / total
    far_lse = jnp.broadcast_to(column + jnp.log2(total), far_out.shape)
    copies[0].wait()
    for slot in range(slots):
        far_here = jnp.where(lengths[slot] > 256, far_lse, neg_fill)
        near = local_lse[slot]
        overall = jnp.maximum(far_here, near)
        a, b = jnp.exp2(far_here - overall), jnp.exp2(near - overall)
        final = ((a * far_out + b * local_out[slot]) / (a + b)).astype(BF16)
        for g in range(groups):
            columns = slice(g * head_dim, (g + 1) * head_dim)
            for half in range(2):
                start = g * steps + half * 2
                result[slot * 2 + half, :, columns] = final[start : start + 2]


VMEM = pl.BlockSpec(memory_space=pltpu.VMEM)
SMEM = pl.BlockSpec(memory_space=pltpu.SMEM)
HBM = pl.BlockSpec(memory_space=pltpu.HBM)


def shards(
    queries, new_keys, new_values, key_cache, value_cache, lengths, block_owner, block_number
):
    slots, steps, groups, head_dim = queries.shape
    blocks, span = key_cache.shape[:2]
    devices = lax.axis_size("serve")
    chunk = 8
    scale2 = head_dim**-0.5 * math.log2(math.e)
    queries = jnp.transpose(queries, (0, 2, 1, 3))
    new_keys = new_keys.reshape(slots, steps, head_dim)
    new_values = new_values.reshape(slots, steps, head_dim)
    key_cache = key_cache.reshape(blocks, span, head_dim)
    value_cache = value_cache.reshape(blocks, span, head_dim)

    along_z = [[4 * z + y for z in range(16)] for y in range(4)]
    along_y = [[4 * z + y for y in range(4)] for z in range(16)]
    exchange = functools.partial(
        lax.all_to_all, axis_name="serve", split_axis=0, concat_axis=0, tiled=True
    )
    in_hbm = functools.partial(pltpu.with_memory_space_constraint, memory_space=pltpu.HBM)
    in_vmem = functools.partial(pltpu.with_memory_space_constraint, memory_space=pltpu.VMEM)
    queries, new_keys, new_values, key_cache, value_cache, lengths, block_owner, block_number = map(
        in_hbm,
        (queries, new_keys, new_values, key_cache, value_cache, lengths, block_owner, block_number),
    )
    small = pltpu.CompilerParams(vmem_limit_bytes=8 << 20)
    message = pl.pallas_call(
        prep_kernel,
        out_shape=jax.ShapeDtypeStruct((16, PAD, head_dim), BF16),
        in_specs=[HBM, HBM],
        out_specs=VMEM,
        scratch_shapes=[
            pltpu.SMEM((slots,), jnp.int32),
            pltpu.VMEM(queries.shape, BF16),
            pltpu.VMEM((PAD, head_dim), F32),
            pltpu.SemaphoreType.DMA((2,)),
        ],
        compiler_params=small,
        name="prep",
    )(lengths, queries)
    keys, table, local_out, local_lse = pl.pallas_call(
        functools.partial(local_kernel, scale2),
        out_shape=(
            pltpu.VMEM(key_cache.shape, BF16),
            jax.ShapeDtypeStruct((256,), jnp.int32),
            jax.ShapeDtypeStruct((slots, PAD, head_dim), F32),
            jax.ShapeDtypeStruct((slots, PAD, head_dim), F32),
        ),
        in_specs=[HBM] * 8,
        out_specs=(VMEM, SMEM, VMEM, VMEM),
        scratch_shapes=[
            pltpu.SMEM((slots,), jnp.int32),
            pltpu.SMEM((blocks,), jnp.int32),
            pltpu.SMEM((blocks,), jnp.int32),
            pltpu.VMEM(queries.shape, BF16),
            pltpu.VMEM(new_keys.shape, BF16),
            pltpu.VMEM(new_values.shape, BF16),
            pltpu.VMEM((slots, PAD, head_dim), F32),
            pltpu.VMEM((span, head_dim), BF16),
            pltpu.SemaphoreType.DMA((8,)),
        ],
        compiler_params=small,
        cost_estimate=pl.CostEstimate(
            flops=1 << 28, bytes_accessed=2 * key_cache.size * 2, transcendentals=1 << 18
        ),
        name="local",
    )(
        lengths, block_owner, block_number, queries, new_keys, new_values, key_cache, value_cache
    )
    column = exchange(message, axis_index_groups=along_z)
    far = exchange(jnp.broadcast_to(column[None], (4,) + column.shape), axis_index_groups=along_y)
    back = pl.pallas_call(
        functools.partial(far_kernel, chunk, scale2),
        out_shape=jax.ShapeDtypeStruct((devices, PAD, head_dim), BF16),
        in_specs=[SMEM, VMEM, VMEM, HBM],
        out_specs=VMEM,
        scratch_shapes=[
            pltpu.VMEM((blocks - 4, span, head_dim), BF16),
            pltpu.SemaphoreType.DMA((blocks - 4,)),
        ],
        compiler_params=small,
        name="far",
    )(table, far.reshape(devices, PAD, head_dim), in_vmem(keys), value_cache)
    back = back.reshape(4, 16, PAD, head_dim)
    row_got = exchange(back, axis_index_groups=along_y)
    onward = pl.pallas_call(
        stage_kernel,
        out_shape=jax.ShapeDtypeStruct((16, PAD, head_dim), BF16),
        in_specs=[VMEM],
        out_specs=VMEM,
        compiler_params=small,
        name="stage",
    )(row_got)
    got = exchange(onward, axis_index_groups=along_z)
    rows_out = pl.pallas_call(
        combine_kernel,
        out_shape=jax.ShapeDtypeStruct((8, 2, groups * head_dim), BF16),
        in_specs=[HBM, VMEM, VMEM, VMEM],
        out_specs=VMEM,
        scratch_shapes=[pltpu.SMEM((slots,), jnp.int32), pltpu.SemaphoreType.DMA((1,))],
        compiler_params=small,
        name="combine",
    )(lengths, got, local_out, local_lse)
    swapped = lax.all_to_all(rows_out, "tensor", split_axis=0, concat_axis=0, tiled=True)
    return jnp.transpose(swapped, (1, 0, 2)).reshape(2, 8 * groups * head_dim)


def solution(mesh):
    placed = (
        P("serve", None, "tensor", None),
        P("serve", None, "tensor", None),
        P("serve", None, "tensor", None),
        P("serve", None, "tensor", None),
        P("serve", None, "tensor", None),
        P("serve"),
        P("serve"),
        P("serve"),
    )
    return jax.shard_map(
        shards, mesh=mesh, in_specs=placed, out_specs=P(("serve", "tensor"), None), check_vma=False
    )
```

time: 96.7 us -> 93 us (0.962)
  blocking collectives: 83 us -> 70 us
  Pallas kernels: 12.4 us -> 16.7 us
  starting transfers between devices: 0 us -> 4.18 us
    all_to_all x1 -> x0, blocking collectives: 11 us -> none  [shards(): exchange(jnp.broadcast_to(column[None], (4,) + column.shape), axis_index_...]
    pallas_call x2 -> x3, Pallas kernels: 7.95 us -> 15.3 us  [the longest x1 7.29 us: shards(): pl.pallas_call(functools.partial(far_kernel, chunk, scale2), out_shape=ja...]
    all_to_all x0 -> x1, starting transfers between devices: none -> 4.18 us  [shards(): exchange(jnp.broadcast_to(column[None], (4,) + column.shape), axis_index_...]
    pallas_call x1, Pallas kernels: 2.42 us -> 0.71 us  [shards(): pl.pallas_call(stage_kernel, out_shape=jax.ShapeDtypeStruct((16, PAD, hea...]
    pallas_call x1, Pallas kernels: 2.01 us -> 0.73 us  [shards(): pl.pallas_call(combine_kernel, out_shape=jax.ShapeDtypeStruct((8, 2, grou...]
    all_to_all x1, blocking collectives: 19 us -> 17.9 us  [shards(): got = exchange(onward, axis_index_groups=along_z)]
  transfers between devices with their start and end apart: 0 -> 1, of which waited for: 0 -> 0; matrix products, arithmetic and copies ran while one was open for 0% -> 0% of each run, Pallas kernels for 0% -> 8%
where the time goes in v3:
time: 93 us; the launch traced here: 92.4 us
  blocking collectives  70 us (75%)
  Pallas kernels  16.7 us (18%)
  starting transfers between devices  4.18 us (4%)
  local copies, waits for them, and re-layouts  1.48 us (2%)
    all_to_all x1, blocking collectives, shards(): column = exchange(message, axis_index_groups=along_z)  27.5 us
    all_to_all x1, blocking collectives, shards(): got = exchange(onward, axis_index_groups=along_z)  17.9 us
    all_to_all x1, blocking collectives, shards(): lax.all_to_all(rows_out, 'tensor', split_axis=0, concat_axis=0, tiled=True)  13.6 us
    all_to_all x1, blocking collectives, shards(): row_got = exchange(back, axis_index_groups=along_y)  11 us
    pallas_call x1, Pallas kernels, shards(): pl.pallas_call(functools.partial(far_kernel, chunk, scale2), out_shape=ja...  7.29 us
    pallas_call x1, Pallas kernels, shards(): pl.pallas_call(functools.partial(local_kernel, scale2), out_shape=(pltpu....  7.19 us
    all_to_all x1, starting transfers between devices, shards(): exchange(jnp.broadcast_to(column[None], (4,) + column.shape), axis_index_...  4.18 us
  transfers between devices with their start and end apart: 1, of which 0 were waited for; matrix products, arithmetic and copies ran while one was open for 0% of the time, Pallas kernels for 8%

profile of v3, /device:TPU:1, one launch (start us, length us, event | category | flops | bytes accessed | tf_op | source)
XLA Modules:
  0.0 92.4 jit_solution(11965473050014929641)
XLA Ops:
  0.0 0.8 prep.1
  0.8 27.5 %all_to_all.25 = bf16[16,32,128]{2,1,0:T(8,128)(2,1)S(1)} all-to-all(bf16[16,32,128]{2,1,0:T(8,128)(2,1)S(1)} %prep.1), channel_id=1, replica_groups={{0,32,64,96,128,160,192,224,256,288,320,352,384,416,448,480},{8,40,72,1..., dimensions={0} | all-to-all | bytes 262144 | tf_op jit(solution)/shard_map/all_to_all | solution.py:359
  28.3 0.9 broadcast_in_dim.2
  29.2 4.2 %all-to-all-start.1 = ((bf16[4,16,32,128]{3,2,1,0:T(8,128)(2,1)}), bf16[4,16,32,128]{3,2,1,0:T(8,128)(2,1)S(1)}, u32[]{:S(2)}, u32[]{:S(2)}) async-start(bf16[4,16,32,128]{3,2,1,0:T(8,128)(2,1)} %broadcast_in_dim.2), calls=%async_computation.1 | async-start | bytes 1048576 | tf_op jit(solution)/shard_map/all_to_all | solution.py:360
  33.4 7.2 %local.1 = (bf16[36,256,128]{2,1,0:T(8,128)(2,1)S(1)}, s32[256]{0:T(256)S(1)}, f32[4,32,128]{2,1,0:T(8,128)S(1)}, f32[4,32,128]{2,1,0:T(8,128)S(1)}) custom-call(s32[4]{0:T(128)} %lengths_hbm.5, s32[36]{0:T(128)} %owners_hbm.1, s32[36]{0:T(128)} %numbers_hbm.1, bf16[4,7,4,128]{3,2,1,0:T(4,128)(2,1)} %bitcast.16, bf16[4,4,128]{2,1,0:T(4,128)(2,1)} %bitcast.18, ...), custom_call_target="tpu_custom_call" | custom-call | flops 268435456 | bytes 4718592 | tf_op jit(solution)/shard_map/local/pallas_call | solution.py:330
  40.6 0.0 all-to-all-done.1
  40.6 7.3 %far.1 = bf16[64,32,128]{2,1,0:T(8,128)(2,1)S(1)} custom-call(s32[256]{0:T(256)S(1)} %get-tuple-element.9.table, bf16[64,32,128]{2,1,0:T(8,128)(2,1)S(1)} %bitcast.10, bf16[36,256,128]{2,1,0:T(8,128)(2,1)S(1)} %get-tuple-element.10.keys, bf16[36,256,128]{2,1,0:T(8,128)(2,1)} %bitcast.13), custom_call_target="tpu_custom_call" | custom-call | tf_op jit(solution)/shard_map/far/pallas_call | solution.py:361
  47.9 11.0 %all_to_all.26.got = bf16[4,16,32,128]{3,2,1,0:T(8,128)(2,1)S(1)} all-to-all(bf16[4,16,32,128]{3,2,1,0:T(8,128)(2,1)S(1)} %bitcast.11), channel_id=1, replica_groups={{0,8,16,24},{32,40,48,56},{64,72,80,88},{96,104,112,120},{128,136,144,1..., dimensions={0} | all-to-all | bytes 1048576 | tf_op jit(solution)/shard_map/all_to_all | solution.py:374
  58.9 0.7 stage.1
  59.6 17.9 %all_to_all.27.got = bf16[16,32,128]{2,1,0:T(8,128)(2,1)S(1)} all-to-all(bf16[16,32,128]{2,1,0:T(8,128)(2,1)S(1)} %stage.1), channel_id=1, replica_groups={{0,32,64,96,128,160,192,224,256,288,320,352,384,416,448,480},{8,40,72,1..., dimensions={0} | all-to-all | bytes 262144 | tf_op jit(solution)/shard_map/all_to_all | solution.py:383
  77.5 0.7 combine.1
  78.2 13.6 %all_to_all.28 = bf16[8,2,896]{2,1,0:T(2,128)(2,1)S(1)} all-to-all(bf16[8,2,896]{2,1,0:T(2,128)(2,1)S(1)} %combine.1), channel_id=1, replica_groups=mesh['serve'=64,'tensor'=8] {'tensor'}, dimensions={0} | all-to-all | bytes 57344 | tf_op jit(solution)/shard_map/all_to_all | solution.py:393
  91.8 0.6 copy.10
Async XLA Ops:
  29.2 11.4 %all-to-all-start.1 = ((bf16[4,16,32,128]{3,2,1,0:T(8,128)(2,1)}), bf16[4,16,32,128]{3,2,1,0:T(8,128)(2,1)S(1)}, u32[]{:S(2)}, u32[]{:S(2)}) async-start(bf16[4,16,32,128]{3,2,1,0:T(8,128)(2,1)} %broadcast_in_dim.2), calls=%async_computation.1 | async-start | bytes 1048576 | tf_op jit(solution)/shard_map/all_to_all | solution.py:360

commit v4 on v3

--- a/solution.py
+++ b/solution.py
@@ -152,7 +152,8 @@
     count = blocks - 4
     me = lax.axis_index("serve")
     far_count = table[192]
-    copies = fetch([(value_cache.at[table[k]], values.at[k]) for k in range(count)], sems)
+    parts = [pl.ds(k * (blocks // 4), blocks // 4) for k in range(4)]
+    copies = fetch([(value_cache.at[part], values.at[part]) for part in parts], sems)
     row, lane = iota((PAD, head_dim), 0), iota((PAD, head_dim), 1)
     offset = lax.bitwise_and(me, 3) * PAD
     diagonal = jnp.logical_and(lane == offset + row, row < rows)
@@ -183,11 +184,13 @@
         total = jnp.sum(weights.astype(F32), axis=1, keepdims=True)
         lse = top * scale2 + jnp.log2(total)
         inverse = 1.0 / total
+        if c == 0:
+            for copy in copies:
+                copy.wait()
         for k in range(chunk):
             part = slice(k * PAD, (k + 1) * PAD)
-            copies[c * chunk + k].wait()
             out = lax.dot_general(
-                weights[part], values[c * chunk + k], (((1,), (0,)), ((), ())),
+                weights[part], values[ids[k]], (((1,), (0,)), ((), ())),
                 preferred_element_type=F32,
             )
             flat = jnp.sum(jnp.where(diagonal, lse[part], 0.0), axis=0, keepdims=True)
@@ -293,7 +296,7 @@
     slots, steps, groups, head_dim = queries.shape
     blocks, span = key_cache.shape[:2]
     devices = lax.axis_size("serve")
-    chunk = 8
+    chunk = 32
     scale2 = head_dim**-0.5 * math.log2(math.e)
     queries = jnp.transpose(queries, (0, 2, 1, 3))
     new_keys = new_keys.reshape(slots, steps, head_dim)
@@ -357,6 +360,7 @@
         lengths, block_owner, block_number, queries, new_keys, new_values, key_cache, value_cache
     )
     column = exchange(message, axis_index_groups=along_z)
+    column, keys, table = lax.optimization_barrier((column, keys, table))
     far = exchange(jnp.broadcast_to(column[None], (4,) + column.shape), axis_index_groups=along_y)
     back = pl.pallas_call(
         functools.partial(far_kernel, chunk, scale2),
@@ -364,8 +368,8 @@
         in_specs=[SMEM, VMEM, VMEM, HBM],
         out_specs=VMEM,
         scratch_shapes=[
-            pltpu.VMEM((blocks - 4, span, head_dim), BF16),
-            pltpu.SemaphoreType.DMA((blocks - 4,)),
+            pltpu.VMEM((blocks, span, head_dim), BF16),
+            pltpu.SemaphoreType.DMA((4,)),
         ],
         compiler_params=small,
         name="far",

time: 93 us -> 88.9 us (0.956)
  blocking collectives: 70 us -> 53.6 us
  starting transfers between devices: 4.18 us -> 15.8 us
  waiting for transfers between devices: 0.01 us -> 4.79 us
  Pallas kernels: 16.7 us -> 13.4 us
    all_to_all x1, blocking collectives: 27.5 us -> 10.9 us  [shards(): exchange(jnp.broadcast_to(column[None], (4,) + column.shape), axis_index_...]
    all_to_all x1, starting transfers between devices: 4.18 us -> 15.8 us  [shards(): column = exchange(message, axis_index_groups=along_z)]
    all_to_all x1, waiting for transfers between devices: 0.01 us -> 4.79 us  [shards(): column = exchange(message, axis_index_groups=along_z)]
    pallas_call x1, Pallas kernels: 7.29 us -> 3.34 us  [shards(): pl.pallas_call(functools.partial(far_kernel, chunk, scale2), out_shape=ja...]
    all_to_all x1, blocking collectives: 11 us -> 9.33 us  [shards(): row_got = exchange(back, axis_index_groups=along_y)]
    all_to_all x1, blocking collectives: 17.9 us -> 19.4 us  [shards(): got = exchange(onward, axis_index_groups=along_z)]
  transfers between devices with their start and end apart: 1 -> 1, of which waited for: 0 -> 1; matrix products, arithmetic and copies ran while one was open for 0% -> 0% of each run, Pallas kernels for 8% -> 8%
where the time goes in v4:
time: 88.9 us; the launch traced here: 88.3 us
  blocking collectives  53.6 us (60%)
  starting transfers between devices  15.8 us (18%)
  Pallas kernels  13.4 us (15%)
  waiting for transfers between devices  4.79 us (5%)
    all_to_all x1, blocking collectives, shards(): got = exchange(onward, axis_index_groups=along_z)  19.4 us
    all_to_all x1, starting transfers between devices, shards(): column = exchange(message, axis_index_groups=along_z)  15.8 us
    all_to_all x1, blocking collectives, shards(): lax.all_to_all(rows_out, 'tensor', split_axis=0, concat_axis=0, tiled=True)  13.9 us
    all_to_all x1, blocking collectives, shards(): exchange(jnp.broadcast_to(column[None], (4,) + column.shape), axis_index_...  10.9 us
    all_to_all x1, blocking collectives, shards(): row_got = exchange(back, axis_index_groups=along_y)  9.33 us
    pallas_call x1, Pallas kernels, shards(): pl.pallas_call(functools.partial(local_kernel, scale2), out_shape=(pltpu....  7.2 us
    all_to_all x1, waiting for transfers between devices, shards(): column = exchange(message, axis_index_groups=along_z)  4.79 us
    pallas_call x1, Pallas kernels, shards(): pl.pallas_call(functools.partial(far_kernel, chunk, scale2), out_shape=ja...  3.34 us
  transfers between devices with their start and end apart: 1, of which 1 were waited for; matrix products, arithmetic and copies ran while one was open for 0% of the time, Pallas kernels for 8%

profile of v4, /device:TPU:1, one launch (start us, length us, event | category | flops | bytes accessed | tf_op | source)
XLA Modules:
  0.0 88.3 jit_solution(16967463271175076896)
XLA Ops:
  0.0 1.4 %prep.1 = bf16[16,32,128]{2,1,0:T(8,128)(2,1)} custom-call(s32[4]{0:T(128)} %lengths_hbm.5, bf16[4,7,4,128]{3,2,1,0:T(4,128)(2,1)} %bitcast.15), custom_call_target="tpu_custom_call" | custom-call | tf_op jit(solution)/shard_map/prep/pallas_call | solution.py:319
  1.4 15.8 %all-to-all-start = ((bf16[16,32,128]{2,1,0:T(8,128)(2,1)}), bf16[16,32,128]{2,1,0:T(8,128)(2,1)S(1)}, u32[]{:S(2)}, u32[]{:S(2)}) async-start(bf16[16,32,128]{2,1,0:T(8,128)(2,1)} %prep.1), calls=%async_computation | async-start | bytes 262144 | tf_op jit(solution)/shard_map/all_to_all | solution.py:362
  17.2 7.2 %local.1 = (bf16[36,256,128]{2,1,0:T(8,128)(2,1)S(1)}, s32[256]{0:T(256)S(1)}, f32[4,32,128]{2,1,0:T(8,128)S(1)}, f32[4,32,128]{2,1,0:T(8,128)S(1)}) custom-call(s32[4]{0:T(128)} %lengths_hbm.5, s32[36]{0:T(128)} %owners_hbm.1, s32[36]{0:T(128)} %numbers_hbm.1, bf16[4,7,4,128]{3,2,1,0:T(4,128)(2,1)} %bitcast.16, bf16[4,4,128]{2,1,0:T(4,128)(2,1)} %bitcast.18, ...), custom_call_target="tpu_custom_call" | custom-call | flops 268435456 | bytes 4718592 | tf_op jit(solution)/shard_map/local/pallas_call | solution.py:333
  24.4 4.8 %all-to-all-done = bf16[16,32,128]{2,1,0:T(8,128)(2,1)S(1)} async-done(((bf16[16,32,128]{2,1,0:T(8,128)(2,1)}), bf16[16,32,128]{2,1,0:T(8,128)(2,1)S(1)}, u32[]{:S(2)}, u32[]{:S(2)}) %all-to-all-start) | async-done | bytes 131104 | tf_op jit(solution)/shard_map/all_to_all | solution.py:362
  29.2 0.1 broadcast_in_dim.2
  29.3 10.9 %all_to_all.25 = bf16[4,16,32,128]{3,2,1,0:T(8,128)(2,1)S(1)} all-to-all(bf16[4,16,32,128]{3,2,1,0:T(8,128)(2,1)S(1)} %broadcast_in_dim.2), channel_id=1, replica_groups={{0,8,16,24},{32,40,48,56},{64,72,80,88},{96,104,112,120},{128,136,144,1..., dimensions={0} | all-to-all | bytes 1048576 | tf_op jit(solution)/shard_map/all_to_all | solution.py:364
  40.2 3.3 %far.1 = bf16[64,32,128]{2,1,0:T(8,128)(2,1)S(1)} custom-call(s32[256]{0:T(256)S(1)} %get-tuple-element.14.table, bf16[64,32,128]{2,1,0:T(8,128)(2,1)S(1)} %bitcast.10, bf16[36,256,128]{2,1,0:T(8,128)(2,1)S(1)} %get-tuple-element.16.keys, bf16[36,256,128]{2,1,0:T(8,128)(2,1)} %bitcast.13), custom_call_target="tpu_custom_call" | custom-call | tf_op jit(solution)/shard_map/far/pallas_call | solution.py:365
  43.5 9.3 %all_to_all.26.got = bf16[4,16,32,128]{3,2,1,0:T(8,128)(2,1)S(1)} all-to-all(bf16[4,16,32,128]{3,2,1,0:T(8,128)(2,1)S(1)} %bitcast.11), channel_id=1, replica_groups={{0,8,16,24},{32,40,48,56},{64,72,80,88},{96,104,112,120},{128,136,144,1..., dimensions={0} | all-to-all | bytes 1048576 | tf_op jit(solution)/shard_map/all_to_all | solution.py:378
  52.9 0.7 stage.1
  53.6 19.4 %all_to_all.27.got = bf16[16,32,128]{2,1,0:T(8,128)(2,1)S(1)} all-to-all(bf16[16,32,128]{2,1,0:T(8,128)(2,1)S(1)} %stage.1), channel_id=1, replica_groups={{0,32,64,96,128,160,192,224,256,288,320,352,384,416,448,480},{8,40,72,1..., dimensions={0} | all-to-all | bytes 262144 | tf_op jit(solution)/shard_map/all_to_all | solution.py:387
  73.0 0.7 combine.1
  73.7 13.9 %all_to_all.28 = bf16[8,2,896]{2,1,0:T(2,128)(2,1)S(1)} all-to-all(bf16[8,2,896]{2,1,0:T(2,128)(2,1)S(1)} %combine.1), channel_id=1, replica_groups=mesh['serve'=64,'tensor'=8] {'tensor'}, dimensions={0} | all-to-all | bytes 57344 | tf_op jit(solution)/shard_map/all_to_all | solution.py:397
  87.7 0.6 copy.10
Async XLA Ops:
  1.4 27.8 %all-to-all-start = ((bf16[16,32,128]{2,1,0:T(8,128)(2,1)}), bf16[16,32,128]{2,1,0:T(8,128)(2,1)S(1)}, u32[]{:S(2)}, u32[]{:S(2)}) async-start(bf16[16,32,128]{2,1,0:T(8,128)(2,1)} %prep.1), calls=%async_computation | async-start | bytes 262144 | tf_op jit(solution)/shard_map/all_to_all | solution.py:362

commit v5 on v4

--- a/solution.py
+++ b/solution.py
@@ -84,30 +84,33 @@
     scale2, lengths_hbm, owners_hbm, numbers_hbm, queries_hbm, new_keys_hbm, new_values_hbm,
     key_cache, value_cache,
     keys, table, local_out, local_lse,
-    lengths, owners, numbers, queries, new_keys, new_values, padded, one_value, sems,
+    lengths, owners, numbers, queries, new_keys, new_values, padded, near_values, sems,
 ):
     blocks, span, head_dim = keys.shape
     slots, steps, _ = new_keys.shape
     me = lax.axis_index("serve")
     small = ((lengths_hbm, lengths), (owners_hbm, owners), (numbers_hbm, numbers),
              (queries_hbm, queries), (new_keys_hbm, new_keys), (new_values_hbm, new_values))
-    copies = fetch(small + ((key_cache, keys),), sems)
-    for copy in copies[: len(small)]:
+    all_keys, *copies = fetch(((key_cache, keys),) + small, sems)
+    for copy in copies:
         copy.wait()
 
-    def place(p, counts):
-        far_count, near_count = counts
-        device = lax.shift_right_logical(owners[p], 2)
+    far_count, near_count = jnp.int32(0), jnp.int32(0)
+    for p in range(blocks):
+        owner, number = owners[p], numbers[p]
+        device = lax.shift_right_logical(owner, 2)
         near = device == me
         at = jnp.where(near, blocks - 1 - near_count, far_count)
         table[at] = p
-        table[64 + at] = jnp.where(near, lax.bitwise_and(owners[p], 3), column_first(device))
-        table[128 + at] = numbers[p] * span
+        table[64 + at] = jnp.where(near, lax.bitwise_and(owner, 3), column_first(device))
+        table[128 + at] = number * span
         one = near.astype(jnp.int32)
-        return far_count + 1 - one, near_count + one
-
-    far_count, near_count = lax.fori_loop(0, blocks, place, (jnp.int32(0), jnp.int32(0)))
+        far_count, near_count = far_count + 1 - one, near_count + one
     table[192] = far_count
+    own_values = fetch(
+        [(value_cache.at[table[blocks - 1 - k]], near_values.at[k]) for k in range(slots)],
+        sems.at[pl.ds(8, slots)],
+    )
 
     for slot in range(slots):
         pad_rows(lengths[slot], queries.at[slot], padded.at[slot])
@@ -125,25 +128,43 @@
     lse = jnp.broadcast_to(top * scale2 + jnp.log2(total), out.shape)
     local_out[...] = (out / total).reshape(local_out.shape)
     local_lse[...] = lse.reshape(local_lse.shape)
-    for copy in copies[len(small) :]:
-        copy.wait()
-
-    def merge(k, carry):
-        p, slot = table[blocks - 1 - k], table[64 + blocks - 1 - k]
-        copy = pltpu.make_async_copy(value_cache.at[p], one_value, sems.at[7])
-        copy.start()
-        copy.wait()
-        limit = (lengths[slot] - table[128 + blocks - 1 - k]).astype(F32)
-        new_out, new = attend(padded[slot].astype(BF16), limit, keys[p], one_value[...], scale2)
-        old, new = local_lse[slot], jnp.broadcast_to(new, new_out.shape)
+
+    def merge(slot, new_out, new):
+        old = local_lse[slot]
         overall = jnp.maximum(old, new)
         a, b = jnp.exp2(old - overall), jnp.exp2(new - overall)
         total = a + b
         local_out[slot] = (a * local_out[slot] + b * new_out) / total
         local_lse[slot] = overall + jnp.log2(total)
+
+    all_keys.wait()
+    for copy in own_values:
+        copy.wait()
+    ats = [blocks - 1 - k for k in range(slots)]
+    parts = []
+    for k, at in enumerate(ats):
+        slot = table[64 + at]
+        limit = (lengths[slot] - table[128 + at]).astype(F32)
+        parts.append(
+            attend(padded[slot].astype(BF16), limit, keys[table[at]], near_values[k], scale2)
+        )
+    for at, (new_out, new) in zip(ats, parts):
+        merge(table[64 + at], new_out, jnp.broadcast_to(new, new_out.shape))
+
+    def more(k, carry):
+        at = blocks - 1 - k
+        slot = table[64 + at]
+        copy = pltpu.make_async_copy(value_cache.at[table[at]], near_values.at[0], sems.at[8])
+        copy.start()
+        copy.wait()
+        limit = (lengths[slot] - table[128 + at]).astype(F32)
+        new_out, new = attend(
+            padded[slot].astype(BF16), limit, keys[table[at]], near_values[0], scale2
+        )
+        merge(slot, new_out, jnp.broadcast_to(new, new_out.shape))
         return carry
 
-    lax.fori_loop(0, near_count, merge, 0)
+    lax.fori_loop(slots, near_count, more, 0)
 
 
 def far_kernel(chunk, scale2, table, far, keys, value_cache, back, values, sems):
@@ -348,8 +369,8 @@
             pltpu.VMEM(new_keys.shape, BF16),
             pltpu.VMEM(new_values.shape, BF16),
             pltpu.VMEM((slots, PAD, head_dim), F32),
-            pltpu.VMEM((span, head_dim), BF16),
-            pltpu.SemaphoreType.DMA((8,)),
+            pltpu.VMEM((slots, span, head_dim), BF16),
+            pltpu.SemaphoreType.DMA((8 + slots,)),
         ],
         compiler_params=small,
         cost_estimate=pl.CostEstimate(

time: 88.9 us -> 88.1 us (level)
  waiting for transfers between devices: 4.79 us -> 7.53 us
  Pallas kernels: 13.4 us -> 10.7 us
    pallas_call x1, Pallas kernels: 7.2 us -> 4.46 us  [shards(): pl.pallas_call(functools.partial(local_kernel, scale2), out_shape=(pltpu....]
    all_to_all x1, waiting for transfers between devices: 4.79 us -> 7.53 us  [shards(): column = exchange(message, axis_index_groups=along_z)]
  transfers between devices with their start and end apart: 1 -> 1, of which waited for: 1 -> 1; matrix products, arithmetic and copies ran while one was open for 0% -> 0% of each run, Pallas kernels for 8% -> 5%
where the time goes in v5:
time: 88.1 us; the launch traced here: 87.6 us
  blocking collectives  52.9 us (60%)
  starting transfers between devices  15.8 us (18%)
  Pallas kernels  10.7 us (12%)
  waiting for transfers between devices  7.53 us (9%)
    all_to_all x1, blocking collectives, shards(): got = exchange(onward, axis_index_groups=along_z)  18.7 us
    all_to_all x1, starting transfers between devices, shards(): column = exchange(message, axis_index_groups=along_z)  15.8 us
    all_to_all x1, blocking collectives, shards(): lax.all_to_all(rows_out, 'tensor', split_axis=0, concat_axis=0, tiled=True)  13.9 us
    all_to_all x1, blocking collectives, shards(): exchange(jnp.broadcast_to(column[None], (4,) + column.shape), axis_index_...  10.9 us
    all_to_all x1, blocking collectives, shards(): row_got = exchange(back, axis_index_groups=along_y)  9.33 us
    all_to_all x1, waiting for transfers between devices, shards(): column = exchange(message, axis_index_groups=along_z)  7.53 us
    pallas_call x1, Pallas kernels, shards(): pl.pallas_call(functools.partial(local_kernel, scale2), out_shape=(pltpu....  4.46 us
    pallas_call x1, Pallas kernels, shards(): pl.pallas_call(functools.partial(far_kernel, chunk, scale2), out_shape=ja...  3.34 us
  transfers between devices with their start and end apart: 1, of which 1 were waited for; matrix products, arithmetic and copies ran while one was open for 0% of the time, Pallas kernels for 5%

profile of v5, /device:TPU:1, one launch (start us, length us, event | category | flops | bytes accessed | tf_op | source)
XLA Modules:
  0.0 87.6 jit_solution(12596666388852295159)
XLA Ops:
  0.0 1.4 %prep.1 = bf16[16,32,128]{2,1,0:T(8,128)(2,1)} custom-call(s32[4]{0:T(128)} %lengths_hbm.5, bf16[4,7,4,128]{3,2,1,0:T(4,128)(2,1)} %bitcast.15), custom_call_target="tpu_custom_call" | custom-call | tf_op jit(solution)/shard_map/prep/pallas_call | solution.py:340
  1.4 15.8 %all-to-all-start = ((bf16[16,32,128]{2,1,0:T(8,128)(2,1)}), bf16[16,32,128]{2,1,0:T(8,128)(2,1)S(1)}, u32[]{:S(2)}, u32[]{:S(2)}) async-start(bf16[16,32,128]{2,1,0:T(8,128)(2,1)} %prep.1), calls=%async_computation | async-start | bytes 262144 | tf_op jit(solution)/shard_map/all_to_all | solution.py:383
  17.2 4.5 %local.1 = (bf16[36,256,128]{2,1,0:T(8,128)(2,1)S(1)}, s32[256]{0:T(256)S(1)}, f32[4,32,128]{2,1,0:T(8,128)S(1)}, f32[4,32,128]{2,1,0:T(8,128)S(1)}) custom-call(s32[4]{0:T(128)} %lengths_hbm.5, s32[36]{0:T(128)} %owners_hbm.1, s32[36]{0:T(128)} %numbers_hbm.1, bf16[4,7,4,128]{3,2,1,0:T(4,128)(2,1)} %bitcast.16, bf16[4,4,128]{2,1,0:T(4,128)(2,1)} %bitcast.18, ...), custom_call_target="tpu_custom_call" | custom-call | flops 268435456 | bytes 4718592 | tf_op jit(solution)/shard_map/local/pallas_call | solution.py:354
  21.7 7.5 %all-to-all-done = bf16[16,32,128]{2,1,0:T(8,128)(2,1)S(1)} async-done(((bf16[16,32,128]{2,1,0:T(8,128)(2,1)}), bf16[16,32,128]{2,1,0:T(8,128)(2,1)S(1)}, u32[]{:S(2)}, u32[]{:S(2)}) %all-to-all-start) | async-done | bytes 131104 | tf_op jit(solution)/shard_map/all_to_all | solution.py:383
  29.2 0.1 broadcast_in_dim.2
  29.3 10.9 %all_to_all.25 = bf16[4,16,32,128]{3,2,1,0:T(8,128)(2,1)S(1)} all-to-all(bf16[4,16,32,128]{3,2,1,0:T(8,128)(2,1)S(1)} %broadcast_in_dim.2), channel_id=1, replica_groups={{0,8,16,24},{32,40,48,56},{64,72,80,88},{96,104,112,120},{128,136,144,1..., dimensions={0} | all-to-all | bytes 1048576 | tf_op jit(solution)/shard_map/all_to_all | solution.py:385
  40.2 3.3 %far.1 = bf16[64,32,128]{2,1,0:T(8,128)(2,1)S(1)} custom-call(s32[256]{0:T(256)S(1)} %get-tuple-element.14.table, bf16[64,32,128]{2,1,0:T(8,128)(2,1)S(1)} %bitcast.10, bf16[36,256,128]{2,1,0:T(8,128)(2,1)S(1)} %get-tuple-element.16.keys, bf16[36,256,128]{2,1,0:T(8,128)(2,1)} %bitcast.13), custom_call_target="tpu_custom_call" | custom-call | tf_op jit(solution)/shard_map/far/pallas_call | solution.py:386
  43.5 9.3 %all_to_all.26.got = bf16[4,16,32,128]{3,2,1,0:T(8,128)(2,1)S(1)} all-to-all(bf16[4,16,32,128]{3,2,1,0:T(8,128)(2,1)S(1)} %bitcast.11), channel_id=1, replica_groups={{0,8,16,24},{32,40,48,56},{64,72,80,88},{96,104,112,120},{128,136,144,1..., dimensions={0} | all-to-all | bytes 1048576 | tf_op jit(solution)/shard_map/all_to_all | solution.py:399
  52.9 0.7 stage.1
  53.6 18.7 %all_to_all.27.got = bf16[16,32,128]{2,1,0:T(8,128)(2,1)S(1)} all-to-all(bf16[16,32,128]{2,1,0:T(8,128)(2,1)S(1)} %stage.1), channel_id=1, replica_groups={{0,32,64,96,128,160,192,224,256,288,320,352,384,416,448,480},{8,40,72,1..., dimensions={0} | all-to-all | bytes 262144 | tf_op jit(solution)/shard_map/all_to_all | solution.py:408
  72.3 0.7 combine.1
  73.0 13.9 %all_to_all.28 = bf16[8,2,896]{2,1,0:T(2,128)(2,1)S(1)} all-to-all(bf16[8,2,896]{2,1,0:T(2,128)(2,1)S(1)} %combine.1), channel_id=1, replica_groups=mesh['serve'=64,'tensor'=8] {'tensor'}, dimensions={0} | all-to-all | bytes 57344 | tf_op jit(solution)/shard_map/all_to_all | solution.py:418
  87.0 0.6 copy.10
Async XLA Ops:
  1.4 27.8 %all-to-all-start = ((bf16[16,32,128]{2,1,0:T(8,128)(2,1)}), bf16[16,32,128]{2,1,0:T(8,128)(2,1)S(1)}, u32[]{:S(2)}, u32[]{:S(2)}) async-start(bf16[16,32,128]{2,1,0:T(8,128)(2,1)} %prep.1), calls=%async_computation | async-start | bytes 262144 | tf_op jit(solution)/shard_map/all_to_all | solution.py:383

commit v6 on v5

--- a/solution.py
+++ b/solution.py
@@ -381,7 +381,6 @@
         lengths, block_owner, block_number, queries, new_keys, new_values, key_cache, value_cache
     )
     column = exchange(message, axis_index_groups=along_z)
-    column, keys, table = lax.optimization_barrier((column, keys, table))
     far = exchange(jnp.broadcast_to(column[None], (4,) + column.shape), axis_index_groups=along_y)
     back = pl.pallas_call(
         functools.partial(far_kernel, chunk, scale2),

time: 88.1 us -> 88.1 us (level)
  blocking collectives: 52.9 us -> 69.4 us
  starting transfers between devices: 15.8 us -> 4.18 us
  waiting for transfers between devices: 7.53 us -> 2.48 us
    all_to_all x1, blocking collectives: 10.9 us -> 27.5 us  [shards(): column = exchange(message, axis_index_groups=along_z)]
    all_to_all x1, starting transfers between devices: 15.8 us -> 4.18 us  [shards(): exchange(jnp.broadcast_to(column[None], (4,) + column.shape), axis_index_...]
    all_to_all x1, waiting for transfers between devices: 7.53 us -> 2.48 us  [shards(): exchange(jnp.broadcast_to(column[None], (4,) + column.shape), axis_index_...]
where the time goes in v6:
time: 88.1 us; the launch traced here: 87.6 us
  blocking collectives  69.4 us (79%)
  Pallas kernels  10 us (11%)
  starting transfers between devices  4.18 us (5%)
  waiting for transfers between devices  2.48 us (3%)
  local copies, waits for them, and re-layouts  1.48 us (2%)
    all_to_all x1, blocking collectives, shards(): column = exchange(message, axis_index_groups=along_z)  27.5 us
    all_to_all x1, blocking collectives, shards(): got = exchange(onward, axis_index_groups=along_z)  18.4 us
    all_to_all x1, blocking collectives, shards(): lax.all_to_all(rows_out, 'tensor', split_axis=0, concat_axis=0, tiled=True)  14.1 us
    all_to_all x1, blocking collectives, shards(): row_got = exchange(back, axis_index_groups=along_y)  9.33 us
    pallas_call x1, Pallas kernels, shards(): pl.pallas_call(functools.partial(local_kernel, scale2), out_shape=(pltpu....  4.45 us
    all_to_all x1, starting transfers between devices, shards(): exchange(jnp.broadcast_to(column[None], (4,) + column.shape), axis_index_...  4.18 us
    pallas_call x1, Pallas kernels, shards(): pl.pallas_call(functools.partial(far_kernel, chunk, scale2), out_shape=ja...  3.34 us
    all_to_all x1, waiting for transfers between devices, shards(): exchange(jnp.broadcast_to(column[None], (4,) + column.shape), axis_index_...  2.48 us
  transfers between devices with their start and end apart: 1, of which 1 were waited for; matrix products, arithmetic and copies ran while one was open for 0% of the time, Pallas kernels for 5%

profile of v6, /device:TPU:1, one launch (start us, length us, event | category | flops | bytes accessed | tf_op | source)
XLA Modules:
  0.0 87.6 jit_solution(8597225478574151552)
XLA Ops:
  0.0 0.8 prep.1
  0.8 27.5 %all_to_all.25 = bf16[16,32,128]{2,1,0:T(8,128)(2,1)S(1)} all-to-all(bf16[16,32,128]{2,1,0:T(8,128)(2,1)S(1)} %prep.1), channel_id=1, replica_groups={{0,32,64,96,128,160,192,224,256,288,320,352,384,416,448,480},{8,40,72,1..., dimensions={0} | all-to-all | bytes 262144 | tf_op jit(solution)/shard_map/all_to_all | solution.py:383
  28.3 0.9 broadcast_in_dim.2
  29.2 4.2 %all-to-all-start.1 = ((bf16[4,16,32,128]{3,2,1,0:T(8,128)(2,1)}), bf16[4,16,32,128]{3,2,1,0:T(8,128)(2,1)S(1)}, u32[]{:S(2)}, u32[]{:S(2)}) async-start(bf16[4,16,32,128]{3,2,1,0:T(8,128)(2,1)} %broadcast_in_dim.2), calls=%async_computation.1 | async-start | bytes 1048576 | tf_op jit(solution)/shard_map/all_to_all | solution.py:384
  33.4 4.4 %local.1 = (bf16[36,256,128]{2,1,0:T(8,128)(2,1)S(1)}, s32[256]{0:T(256)S(1)}, f32[4,32,128]{2,1,0:T(8,128)S(1)}, f32[4,32,128]{2,1,0:T(8,128)S(1)}) custom-call(s32[4]{0:T(128)} %lengths_hbm.5, s32[36]{0:T(128)} %owners_hbm.1, s32[36]{0:T(128)} %numbers_hbm.1, bf16[4,7,4,128]{3,2,1,0:T(4,128)(2,1)} %bitcast.16, bf16[4,4,128]{2,1,0:T(4,128)(2,1)} %bitcast.18, ...), custom_call_target="tpu_custom_call" | custom-call | flops 268435456 | bytes 4718592 | tf_op jit(solution)/shard_map/local/pallas_call | solution.py:354
  37.8 2.5 %all-to-all-done.1 = bf16[4,16,32,128]{3,2,1,0:T(8,128)(2,1)S(1)} async-done(((bf16[4,16,32,128]{3,2,1,0:T(8,128)(2,1)}), bf16[4,16,32,128]{3,2,1,0:T(8,128)(2,1)S(1)}, u32[]{:S(2)}, u32[]{:S(2)}) %all-to-all-start.1) | async-done | bytes 524320 | tf_op jit(solution)/shard_map/all_to_all | solution.py:384
  40.3 3.3 %far.1 = bf16[64,32,128]{2,1,0:T(8,128)(2,1)S(1)} custom-call(s32[256]{0:T(256)S(1)} %get-tuple-element.9.table, bf16[64,32,128]{2,1,0:T(8,128)(2,1)S(1)} %bitcast.10, bf16[36,256,128]{2,1,0:T(8,128)(2,1)S(1)} %get-tuple-element.10.keys, bf16[36,256,128]{2,1,0:T(8,128)(2,1)} %bitcast.13), custom_call_target="tpu_custom_call" | custom-call | tf_op jit(solution)/shard_map/far/pallas_call | solution.py:385
  43.7 9.3 %all_to_all.26.got = bf16[4,16,32,128]{3,2,1,0:T(8,128)(2,1)S(1)} all-to-all(bf16[4,16,32,128]{3,2,1,0:T(8,128)(2,1)S(1)} %bitcast.11), channel_id=1, replica_groups={{0,8,16,24},{32,40,48,56},{64,72,80,88},{96,104,112,120},{128,136,144,1..., dimensions={0} | all-to-all | bytes 1048576 | tf_op jit(solution)/shard_map/all_to_all | solution.py:398
  53.0 0.7 stage.1
  53.7 18.4 %all_to_all.27.got = bf16[16,32,128]{2,1,0:T(8,128)(2,1)S(1)} all-to-all(bf16[16,32,128]{2,1,0:T(8,128)(2,1)S(1)} %stage.1), channel_id=1, replica_groups={{0,32,64,96,128,160,192,224,256,288,320,352,384,416,448,480},{8,40,72,1..., dimensions={0} | all-to-all | bytes 262144 | tf_op jit(solution)/shard_map/all_to_all | solution.py:407
  72.1 0.7 combine.1
  72.9 14.1 %all_to_all.28 = bf16[8,2,896]{2,1,0:T(2,128)(2,1)S(1)} all-to-all(bf16[8,2,896]{2,1,0:T(2,128)(2,1)S(1)} %combine.1), channel_id=1, replica_groups=mesh['serve'=64,'tensor'=8] {'tensor'}, dimensions={0} | all-to-all | bytes 57344 | tf_op jit(solution)/shard_map/all_to_all | solution.py:417
  87.0 0.6 copy.10
Async XLA Ops:
  29.2 11.1 %all-to-all-start.1 = ((bf16[4,16,32,128]{3,2,1,0:T(8,128)(2,1)}), bf16[4,16,32,128]{3,2,1,0:T(8,128)(2,1)S(1)}, u32[]{:S(2)}, u32[]{:S(2)}) async-start(bf16[4,16,32,128]{3,2,1,0:T(8,128)(2,1)} %broadcast_in_dim.2), calls=%async_computation.1 | async-start | bytes 1048576 | tf_op jit(solution)/shard_map/all_to_all | solution.py:384

commit v7 on v6

--- a/solution.py
+++ b/solution.py
@@ -83,15 +83,15 @@
 def local_kernel(
     scale2, lengths_hbm, owners_hbm, numbers_hbm, queries_hbm, new_keys_hbm, new_values_hbm,
     key_cache, value_cache,
-    keys, table, local_out, local_lse,
-    lengths, owners, numbers, queries, new_keys, new_values, padded, near_values, sems,
+    table, local_out, local_lse,
+    lengths, owners, numbers, queries, new_keys, new_values, padded, near_keys, near_values, sems,
 ):
-    blocks, span, head_dim = keys.shape
+    blocks, span, head_dim = key_cache.shape
     slots, steps, _ = new_keys.shape
     me = lax.axis_index("serve")
     small = ((lengths_hbm, lengths), (owners_hbm, owners), (numbers_hbm, numbers),
              (queries_hbm, queries), (new_keys_hbm, new_keys), (new_values_hbm, new_values))
-    all_keys, *copies = fetch(((key_cache, keys),) + small, sems)
+    copies = fetch(small, sems)
     for copy in copies:
         copy.wait()
 
@@ -107,9 +107,12 @@
         one = near.astype(jnp.int32)
         far_count, near_count = far_count + 1 - one, near_count + one
     table[192] = far_count
-    own_values = fetch(
-        [(value_cache.at[table[blocks - 1 - k]], near_values.at[k]) for k in range(slots)],
-        sems.at[pl.ds(8, slots)],
+    for slot in range(slots):
+        table[193 + slot] = lengths[slot]
+    own_blocks = fetch(
+        [(key_cache.at[table[blocks - 1 - k]], near_keys.at[k]) for k in range(slots)]
+        + [(value_cache.at[table[blocks - 1 - k]], near_values.at[k]) for k in range(slots)],
+        sems.at[pl.ds(8, 2 * slots)],
     )
 
     for slot in range(slots):
@@ -137,8 +140,7 @@
         local_out[slot] = (a * local_out[slot] + b * new_out) / total
         local_lse[slot] = overall + jnp.log2(total)
 
-    all_keys.wait()
-    for copy in own_values:
+    for copy in own_blocks:
         copy.wait()
     ats = [blocks - 1 - k for k in range(slots)]
     parts = []
@@ -146,7 +148,7 @@
         slot = table[64 + at]
         limit = (lengths[slot] - table[128 + at]).astype(F32)
         parts.append(
-            attend(padded[slot].astype(BF16), limit, keys[table[at]], near_values[k], scale2)
+            attend(padded[slot].astype(BF16), limit, near_keys[k], near_values[k], scale2)
         )
     for at, (new_out, new) in zip(ats, parts):
         merge(table[64 + at], new_out, jnp.broadcast_to(new, new_out.shape))
@@ -154,12 +156,13 @@
     def more(k, carry):
         at = blocks - 1 - k
         slot = table[64 + at]
-        copy = pltpu.make_async_copy(value_cache.at[table[at]], near_values.at[0], sems.at[8])
-        copy.start()
-        copy.wait()
+        block = table[at]
+        pair = ((key_cache.at[block], near_keys.at[0]), (value_cache.at[block], near_values.at[0]))
+        for copy in fetch(pair, sems.at[pl.ds(8, 2)]):
+            copy.wait()
         limit = (lengths[slot] - table[128 + at]).astype(F32)
         new_out, new = attend(
-            padded[slot].astype(BF16), limit, keys[table[at]], near_values[0], scale2
+            padded[slot].astype(BF16), limit, near_keys[0], near_values[0], scale2
         )
         merge(slot, new_out, jnp.broadcast_to(new, new_out.shape))
         return carry
@@ -167,14 +170,12 @@
     lax.fori_loop(slots, near_count, more, 0)
 
 
-def far_kernel(chunk, scale2, table, far, keys, value_cache, back, values, sems):
+def far_kernel(chunk, scale2, table, far, keys, values, back):
     blocks, span, head_dim = keys.shape
     rows = 28
     count = blocks - 4
     me = lax.axis_index("serve")
     far_count = table[192]
-    parts = [pl.ds(k * (blocks // 4), blocks // 4) for k in range(4)]
-    copies = fetch([(value_cache.at[part], values.at[part]) for part in parts], sems)
     row, lane = iota((PAD, head_dim), 0), iota((PAD, head_dim), 1)
     offset = lax.bitwise_and(me, 3) * PAD
     diagonal = jnp.logical_and(lane == offset + row, row < rows)
@@ -205,9 +206,6 @@
         total = jnp.sum(weights.astype(F32), axis=1, keepdims=True)
         lse = top * scale2 + jnp.log2(total)
         inverse = 1.0 / total
-        if c == 0:
-            for copy in copies:
-                copy.wait()
         for k in range(chunk):
             part = slice(k * PAD, (k + 1) * PAD)
             out = lax.dot_general(
@@ -217,6 +215,11 @@
             flat = jnp.sum(jnp.where(diagonal, lse[part], 0.0), axis=0, keepdims=True)
             back[places[k]] = message_of(out * inverse[part], flat, rows)
     back[unused] = empty
+
+
+def spread_kernel(column, copies):
+    for k in range(copies.shape[0]):
+        copies[k] = column[...]
 
 
 def four_fold(x, op):
@@ -257,8 +260,7 @@
         onward[m] = message_of(out[:PAD] + out[PAD:], lse[m : m + 1], rows)
 
 
-def combine_kernel(lengths_hbm, got, local_out, local_lse, result, lengths, sems):
-    copies = fetch(((lengths_hbm, lengths),), sems)
+def combine_kernel(table, got, local_out, local_lse, result):
     devices, _, head_dim = got.shape
     slots = local_out.shape[0]
     steps, groups, rows = 4, 7, 28
@@ -292,9 +294,8 @@
     column = jnp.sum(jnp.where(first, top[0:1], 0.0), axis=1, keepdims=True)
     far_out = out / total
     far_lse = jnp.broadcast_to(column + jnp.log2(total), far_out.shape)
-    copies[0].wait()
     for slot in range(slots):
-        far_here = jnp.where(lengths[slot] > 256, far_lse, neg_fill)
+        far_here = jnp.where(table[193 + slot] > 256, far_lse, neg_fill)
         near = local_lse[slot]
         overall = jnp.maximum(far_here, near)
         a, b = jnp.exp2(far_here - overall), jnp.exp2(near - overall)
@@ -331,7 +332,9 @@
         lax.all_to_all, axis_name="serve", split_axis=0, concat_axis=0, tiled=True
     )
     in_hbm = functools.partial(pltpu.with_memory_space_constraint, memory_space=pltpu.HBM)
+    in_smem = functools.partial(pltpu.with_memory_space_constraint, memory_space=pltpu.SMEM)
     in_vmem = functools.partial(pltpu.with_memory_space_constraint, memory_space=pltpu.VMEM)
+    plain_keys, plain_values = key_cache, value_cache
     queries, new_keys, new_values, key_cache, value_cache, lengths, block_owner, block_number = map(
         in_hbm,
         (queries, new_keys, new_values, key_cache, value_cache, lengths, block_owner, block_number),
@@ -351,16 +354,15 @@
         compiler_params=small,
         name="prep",
     )(lengths, queries)
-    keys, table, local_out, local_lse = pl.pallas_call(
+    table, local_out, local_lse = pl.pallas_call(
         functools.partial(local_kernel, scale2),
         out_shape=(
-            pltpu.VMEM(key_cache.shape, BF16),
-            jax.ShapeDtypeStruct((256,), jnp.int32),
+            pltpu.SMEM((256,), jnp.int32),
             jax.ShapeDtypeStruct((slots, PAD, head_dim), F32),
             jax.ShapeDtypeStruct((slots, PAD, head_dim), F32),
         ),
         in_specs=[HBM] * 8,
-        out_specs=(VMEM, SMEM, VMEM, VMEM),
+        out_specs=(SMEM, VMEM, VMEM),
         scratch_shapes=[
             pltpu.SMEM((slots,), jnp.int32),
             pltpu.SMEM((blocks,), jnp.int32),
@@ -370,30 +372,39 @@
             pltpu.VMEM(new_values.shape, BF16),
             pltpu.VMEM((slots, PAD, head_dim), F32),
             pltpu.VMEM((slots, span, head_dim), BF16),
-            pltpu.SemaphoreType.DMA((8 + slots,)),
+            pltpu.VMEM((slots, span, head_dim), BF16),
+            pltpu.SemaphoreType.DMA((8 + 2 * slots,)),
         ],
         compiler_params=small,
         cost_estimate=pl.CostEstimate(
-            flops=1 << 28, bytes_accessed=2 * key_cache.size * 2, transcendentals=1 << 18
+            flops=1 << 28, bytes_accessed=key_cache.size * 2, transcendentals=1 << 18
         ),
         name="local",
     )(
         lengths, block_owner, block_number, queries, new_keys, new_values, key_cache, value_cache
     )
     column = exchange(message, axis_index_groups=along_z)
-    far = exchange(jnp.broadcast_to(column[None], (4,) + column.shape), axis_index_groups=along_y)
+    column, local_out = lax.optimization_barrier((column, local_out))
+    copies = pl.pallas_call(
+        spread_kernel,
+        out_shape=jax.ShapeDtypeStruct((4,) + column.shape, BF16),
+        in_specs=[VMEM],
+        out_specs=VMEM,
+        compiler_params=small,
+        cost_estimate=pl.CostEstimate(
+            flops=1 << 32, bytes_accessed=1 << 20, transcendentals=0
+        ),
+        name="spread",
+    )(column)
+    far = exchange(copies, axis_index_groups=along_y)
     back = pl.pallas_call(
         functools.partial(far_kernel, chunk, scale2),
         out_shape=jax.ShapeDtypeStruct((devices, PAD, head_dim), BF16),
-        in_specs=[SMEM, VMEM, VMEM, HBM],
+        in_specs=[SMEM, VMEM, VMEM, VMEM],
         out_specs=VMEM,
-        scratch_shapes=[
-            pltpu.VMEM((blocks, span, head_dim), BF16),
-            pltpu.SemaphoreType.DMA((4,)),
-        ],
         compiler_params=small,
         name="far",
-    )(table, far.reshape(devices, PAD, head_dim), in_vmem(keys), value_cache)
+    )(in_smem(table), far.reshape(devices, PAD, head_dim), in_vmem(plain_keys), in_vmem(plain_values))
     back = back.reshape(4, 16, PAD, head_dim)
     row_got = exchange(back, axis_index_groups=along_y)
     onward = pl.pallas_call(
@@ -408,12 +419,11 @@
     rows_out = pl.pallas_call(
         combine_kernel,
         out_shape=jax.ShapeDtypeStruct((8, 2, groups * head_dim), BF16),
-        in_specs=[HBM, VMEM, VMEM, VMEM],
+        in_specs=[SMEM, VMEM, VMEM, VMEM],
         out_specs=VMEM,
-        scratch_shapes=[pltpu.SMEM((slots,), jnp.int32), pltpu.SemaphoreType.DMA((1,))],
         compiler_params=small,
         name="combine",
-    )(lengths, got, local_out, local_lse)
+    )(in_smem(table), got, local_out, local_lse)
     swapped = lax.all_to_all(rows_out, "tensor", split_axis=0, concat_axis=0, tiled=True)
     return jnp.transpose(swapped, (1, 0, 2)).reshape(2, 8 * groups * head_dim)
 

time: 88.1 us -> 85.8 us (0.974)
  blocking collectives: 69.4 us -> 53.1 us
  starting transfers between devices: 4.18 us -> 15.8 us
  waiting for transfers between devices: 2.48 us -> 8.68 us
  Pallas kernels: 10 us -> 7.12 us
    all_to_all x1, blocking collectives: 27.5 us -> 11.2 us  [shards(): far = exchange(copies, axis_index_groups=along_y)]
    all_to_all x1, starting transfers between devices: 4.18 us -> 15.8 us  [shards(): column = exchange(message, axis_index_groups=along_z)]
    all_to_all x1, waiting for transfers between devices: 2.48 us -> 8.68 us  [shards(): column = exchange(message, axis_index_groups=along_z)]
    pallas_call x1, Pallas kernels: 3.34 us -> 1.15 us  [shards(): pl.pallas_call(functools.partial(far_kernel, chunk, scale2), out_shape=ja...]
    pallas_call x1, Pallas kernels: 4.45 us -> 3.31 us  [shards(): pl.pallas_call(functools.partial(local_kernel, scale2), out_shape=(pltpu....]
  transfers between devices with their start and end apart: 1 -> 1, of which waited for: 1 -> 1; matrix products, arithmetic and copies ran while one was open for 0% -> 0% of each run, Pallas kernels for 5% -> 4%
where the time goes in v7:
time: 85.8 us; the launch traced here: 85.4 us
  blocking collectives  53.1 us (62%)
  starting transfers between devices  15.8 us (18%)
  waiting for transfers between devices  8.68 us (10%)
  Pallas kernels  7.12 us (8%)
    all_to_all x1, blocking collectives, shards(): got = exchange(onward, axis_index_groups=along_z)  18.7 us
    all_to_all x1, starting transfers between devices, shards(): column = exchange(message, axis_index_groups=along_z)  15.8 us
    all_to_all x1, blocking collectives, shards(): lax.all_to_all(rows_out, 'tensor', split_axis=0, concat_axis=0, tiled=True)  13.9 us
    all_to_all x1, blocking collectives, shards(): far = exchange(copies, axis_index_groups=along_y)  11.2 us
    all_to_all x1, blocking collectives, shards(): row_got = exchange(back, axis_index_groups=along_y)  9.33 us
    all_to_all x1, waiting for transfers between devices, shards(): column = exchange(message, axis_index_groups=along_z)  8.68 us
    pallas_call x1, Pallas kernels, shards(): pl.pallas_call(functools.partial(local_kernel, scale2), out_shape=(pltpu....  3.31 us
  transfers between devices with their start and end apart: 1, of which 1 were waited for; matrix products, arithmetic and copies ran while one was open for 0% of the time, Pallas kernels for 4%

profile of v7, /device:TPU:1, one launch (start us, length us, event | category | flops | bytes accessed | tf_op | source)
XLA Modules:
  0.0 85.4 jit_solution(4650045599551646)
XLA Ops:
  0.0 1.4 %prep.1 = bf16[16,32,128]{2,1,0:T(8,128)(2,1)} custom-call(s32[4]{0:T(128)} %lengths_hbm.3, bf16[4,7,4,128]{3,2,1,0:T(4,128)(2,1)} %bitcast.16), custom_call_target="tpu_custom_call" | custom-call | tf_op jit(solution)/shard_map/prep/pallas_call | solution.py:343
  1.4 15.8 %all-to-all-start = ((bf16[16,32,128]{2,1,0:T(8,128)(2,1)}), bf16[16,32,128]{2,1,0:T(8,128)(2,1)S(1)}, u32[]{:S(2)}, u32[]{:S(2)}) async-start(bf16[16,32,128]{2,1,0:T(8,128)(2,1)} %prep.1), calls=%async_computation | async-start | bytes 262144 | tf_op jit(solution)/shard_map/all_to_all | solution.py:386
  17.2 3.3 %local.1 = (s32[256]{0:T(256)S(4)}, f32[4,32,128]{2,1,0:T(8,128)S(1)}, f32[4,32,128]{2,1,0:T(8,128)S(1)}) custom-call(s32[4]{0:T(128)} %lengths_hbm.3, s32[36]{0:T(128)} %owners_hbm.1, s32[36]{0:T(128)} %numbers_hbm.1, bf16[4,7,4,128]{3,2,1,0:T(4,128)(2,1)} %bitcast.17, bf16[4,4,128]{2,1,0:T(4,128)(2,1)} %bitcast.19, bf16[4,4,128]{2,1,0:T(4,128)(2,1)} %bitcast.20, ...), custom_call_target="tpu_custom_call" | custom-call | flops 268435456 | bytes 2359296 | tf_op jit(solution)/shard_map/local/pallas_call | solution.py:357
  20.5 8.7 %all-to-all-done.column = bf16[16,32,128]{2,1,0:T(8,128)(2,1)S(1)} async-done(((bf16[16,32,128]{2,1,0:T(8,128)(2,1)}), bf16[16,32,128]{2,1,0:T(8,128)(2,1)S(1)}, u32[]{:S(2)}, u32[]{:S(2)}) %all-to-all-start) | async-done | bytes 131104 | tf_op jit(solution)/shard_map/all_to_all | solution.py:386
  29.2 0.0 copy-start
  29.2 0.0 copy-start.1
  29.2 0.1 spread.1
  29.3 11.2 %all_to_all.25 = bf16[4,16,32,128]{3,2,1,0:T(8,128)(2,1)S(1)} all-to-all(bf16[4,16,32,128]{3,2,1,0:T(8,128)(2,1)S(1)} %spread.1), channel_id=1, replica_groups={{0,8,16,24},{32,40,48,56},{64,72,80,88},{96,104,112,120},{128,136,144,1..., dimensions={0} | all-to-all | bytes 1048576 | tf_op jit(solution)/shard_map/all_to_all | solution.py:399
  40.5 0.0 copy-done
  40.5 0.0 copy-done.1
  40.5 1.2 %far.1 = bf16[64,32,128]{2,1,0:T(8,128)(2,1)S(1)} custom-call(s32[256]{0:T(256)S(4)} %get-tuple-element.10.table, bf16[64,32,128]{2,1,0:T(8,128)(2,1)S(1)} %bitcast.14, bf16[36,256,128]{2,1,0:T(8,128)(2,1)S(1)} %bitcast.11, bf16[36,256,128]{2,1,0:T(8,128)(2,1)S(1)} %bitcast.13), custom_call_target="tpu_custom_call" | custom-call | tf_op jit(solution)/shard_map/far/pallas_call | solution.py:400
  41.6 9.3 %all_to_all.26.got = bf16[4,16,32,128]{3,2,1,0:T(8,128)(2,1)S(1)} all-to-all(bf16[4,16,32,128]{3,2,1,0:T(8,128)(2,1)S(1)} %bitcast.15), channel_id=1, replica_groups={{0,8,16,24},{32,40,48,56},{64,72,80,88},{96,104,112,120},{128,136,144,1..., dimensions={0} | all-to-all | bytes 1048576 | tf_op jit(solution)/shard_map/all_to_all | solution.py:409
  51.0 0.7 stage.1
  51.7 18.7 %all_to_all.27.got = bf16[16,32,128]{2,1,0:T(8,128)(2,1)S(1)} all-to-all(bf16[16,32,128]{2,1,0:T(8,128)(2,1)S(1)} %stage.1), channel_id=1, replica_groups={{0,32,64,96,128,160,192,224,256,288,320,352,384,416,448,480},{8,40,72,1..., dimensions={0} | all-to-all | bytes 262144 | tf_op jit(solution)/shard_map/all_to_all | solution.py:418
  70.4 0.4 combine.1
  70.8 13.9 %all_to_all.28 = bf16[8,2,896]{2,1,0:T(2,128)(2,1)S(1)} all-to-all(bf16[8,2,896]{2,1,0:T(2,128)(2,1)S(1)} %combine.1), channel_id=1, replica_groups=mesh['serve'=64,'tensor'=8] {'tensor'}, dimensions={0} | all-to-all | bytes 57344 | tf_op jit(solution)/shard_map/all_to_all | solution.py:427
  84.8 0.6 copy.10
Async XLA Ops:
  1.4 27.8 %all-to-all-start = ((bf16[16,32,128]{2,1,0:T(8,128)(2,1)}), bf16[16,32,128]{2,1,0:T(8,128)(2,1)S(1)}, u32[]{:S(2)}, u32[]{:S(2)}) async-start(bf16[16,32,128]{2,1,0:T(8,128)(2,1)} %prep.1), calls=%async_computation | async-start | bytes 262144 | tf_op jit(solution)/shard_map/all_to_all | solution.py:386
  29.2 11.3 %copy-start = (bf16[36,256,1,128]{3,1,2,0:T(8,128)(2,1)S(1)}, bf16[36,256,1,128]{3,1,2,0:T(8,128)(2,1)}, u32[]{:S(2)}) copy-start(bf16[36,256,1,128]{3,1,2,0:T(8,128)(2,1)} %param.11) | copy-start | bytes 7077892
  29.2 11.3 %copy-start.1 = (bf16[36,256,1,128]{3,1,2,0:T(8,128)(2,1)S(1)}, bf16[36,256,1,128]{3,1,2,0:T(8,128)(2,1)}, u32[]{:S(2)}) copy-start(bf16[36,256,1,128]{3,1,2,0:T(8,128)(2,1)} %param.12) | copy-start | bytes 7077892

commit v8 on v7

--- a/solution.py
+++ b/solution.py
@@ -227,19 +227,21 @@
     return op(x, pltpu.roll(x, PAD, 1))
 
 
+def gathered_lse(groups, rows):
+    part = iota(groups[0][0].shape, 0) + PAD // 2
+    in_row = jnp.logical_and(part >= rows, part < rows + 3)
+    out = []
+    for group in groups:
+        stats = sum(lower.astype(F32) for lower in group)
+        out.append(jnp.sum(jnp.where(in_row, stats, 0.0), axis=0, keepdims=True))
+    return jnp.concatenate(out, axis=0)
+
+
 def stage_kernel(got, onward):
     sources, many, _, head_dim = got.shape
     rows = 28
     me = lax.axis_index("serve")
-    depth = sources * many * PAD
-    flat = got[...].reshape(depth, head_dim)
-    g2, k2 = iota((many, depth), 0), iota((many, depth), 1)
-    in_row = jnp.logical_and(k2 % PAD >= rows, k2 % PAD < rows + 3)
-    pick = jnp.logical_and((k2 // PAD) % many == g2, in_row)
-    lse = lax.dot_general(
-        jnp.where(pick, 1.0, 0.0).astype(BF16), flat, (((1,), (0,)), ((), ())),
-        preferred_element_type=F32,
-    )
+    lse = gathered_lse([[got[k, m, PAD // 2 :, :] for k in range(sources)] for m in range(many)], rows)
     top = four_fold(lse, jnp.maximum)
     weight = jnp.exp2(lse - top)
     total = four_fold(weight, jnp.add)
@@ -267,12 +269,8 @@
     depth = devices * PAD
     many = devices // 4
     flat = got[...].reshape(depth, head_dim)
-    g2, k2 = iota((many, depth), 0), iota((many, depth), 1)
-    in_row = jnp.logical_and(k2 % PAD >= rows, k2 % PAD < rows + 3)
-    pick = jnp.logical_and(k2 // (4 * PAD) == g2, in_row)
-    lse = lax.dot_general(
-        jnp.where(pick, 1.0, 0.0).astype(BF16), flat, (((1,), (0,)), ((), ())),
-        preferred_element_type=F32,
+    lse = gathered_lse(
+        [[got[4 * g + k, PAD // 2 :, :] for k in range(4)] for g in range(many)], rows
     )
     top = jnp.max(lse, axis=0, keepdims=True)
     top = jnp.broadcast_to(top, (8, head_dim))

time: 85.8 us -> 85.6 us (level)
  no operation moved by 1% of the time
where the time goes in v8:
time: 85.6 us; the launch traced here: 85.1 us
  blocking collectives  53.1 us (62%)
  starting transfers between devices  15.8 us (18%)
  waiting for transfers between devices  8.68 us (10%)
  Pallas kernels  6.83 us (8%)
    all_to_all x1, blocking collectives, shards(): got = exchange(onward, axis_index_groups=along_z)  18.7 us
    all_to_all x1, starting transfers between devices, shards(): column = exchange(message, axis_index_groups=along_z)  15.8 us
    all_to_all x1, blocking collectives, shards(): lax.all_to_all(rows_out, 'tensor', split_axis=0, concat_axis=0, tiled=True)  13.9 us
    all_to_all x1, blocking collectives, shards(): far = exchange(copies, axis_index_groups=along_y)  11.2 us
    all_to_all x1, blocking collectives, shards(): row_got = exchange(back, axis_index_groups=along_y)  9.33 us
    all_to_all x1, waiting for transfers between devices, shards(): column = exchange(message, axis_index_groups=along_z)  8.68 us
    pallas_call x1, Pallas kernels, shards(): pl.pallas_call(functools.partial(local_kernel, scale2), out_shape=(pltpu....  3.31 us
  transfers between devices with their start and end apart: 1, of which 1 were waited for; matrix products, arithmetic and copies ran while one was open for 0% of the time, Pallas kernels for 4%

profile of v8, /device:TPU:1, one launch (start us, length us, event | category | flops | bytes accessed | tf_op | source)
XLA Modules:
  0.0 85.1 jit_solution(17508581528062267364)
XLA Ops:
  0.0 1.4 %prep.1 = bf16[16,32,128]{2,1,0:T(8,128)(2,1)} custom-call(s32[4]{0:T(128)} %lengths_hbm.3, bf16[4,7,4,128]{3,2,1,0:T(4,128)(2,1)} %bitcast.16), custom_call_target="tpu_custom_call" | custom-call | tf_op jit(solution)/shard_map/prep/pallas_call | solution.py:341
  1.4 15.8 %all-to-all-start = ((bf16[16,32,128]{2,1,0:T(8,128)(2,1)}), bf16[16,32,128]{2,1,0:T(8,128)(2,1)S(1)}, u32[]{:S(2)}, u32[]{:S(2)}) async-start(bf16[16,32,128]{2,1,0:T(8,128)(2,1)} %prep.1), calls=%async_computation | async-start | bytes 262144 | tf_op jit(solution)/shard_map/all_to_all | solution.py:384
  17.2 3.3 %local.1 = (s32[256]{0:T(256)S(4)}, f32[4,32,128]{2,1,0:T(8,128)S(1)}, f32[4,32,128]{2,1,0:T(8,128)S(1)}) custom-call(s32[4]{0:T(128)} %lengths_hbm.3, s32[36]{0:T(128)} %owners_hbm.1, s32[36]{0:T(128)} %numbers_hbm.1, bf16[4,7,4,128]{3,2,1,0:T(4,128)(2,1)} %bitcast.17, bf16[4,4,128]{2,1,0:T(4,128)(2,1)} %bitcast.19, bf16[4,4,128]{2,1,0:T(4,128)(2,1)} %bitcast.20, ...), custom_call_target="tpu_custom_call" | custom-call | flops 268435456 | bytes 2359296 | tf_op jit(solution)/shard_map/local/pallas_call | solution.py:355
  20.5 8.7 %all-to-all-done.column = bf16[16,32,128]{2,1,0:T(8,128)(2,1)S(1)} async-done(((bf16[16,32,128]{2,1,0:T(8,128)(2,1)}), bf16[16,32,128]{2,1,0:T(8,128)(2,1)S(1)}, u32[]{:S(2)}, u32[]{:S(2)}) %all-to-all-start) | async-done | bytes 131104 | tf_op jit(solution)/shard_map/all_to_all | solution.py:384
  29.2 0.0 copy-start
  29.2 0.0 copy-start.1
  29.2 0.1 spread.1
  29.3 11.2 %all_to_all.25 = bf16[4,16,32,128]{3,2,1,0:T(8,128)(2,1)S(1)} all-to-all(bf16[4,16,32,128]{3,2,1,0:T(8,128)(2,1)S(1)} %spread.1), channel_id=1, replica_groups={{0,8,16,24},{32,40,48,56},{64,72,80,88},{96,104,112,120},{128,136,144,1..., dimensions={0} | all-to-all | bytes 1048576 | tf_op jit(solution)/shard_map/all_to_all | solution.py:397
  40.5 0.0 copy-done
  40.5 0.0 copy-done.1
  40.5 1.2 %far.1 = bf16[64,32,128]{2,1,0:T(8,128)(2,1)S(1)} custom-call(s32[256]{0:T(256)S(4)} %get-tuple-element.10.table, bf16[64,32,128]{2,1,0:T(8,128)(2,1)S(1)} %bitcast.14, bf16[36,256,128]{2,1,0:T(8,128)(2,1)S(1)} %bitcast.11, bf16[36,256,128]{2,1,0:T(8,128)(2,1)S(1)} %bitcast.13), custom_call_target="tpu_custom_call" | custom-call | tf_op jit(solution)/shard_map/far/pallas_call | solution.py:398
  41.6 9.3 %all_to_all.26.got = bf16[4,16,32,128]{3,2,1,0:T(8,128)(2,1)S(1)} all-to-all(bf16[4,16,32,128]{3,2,1,0:T(8,128)(2,1)S(1)} %bitcast.15), channel_id=1, replica_groups={{0,8,16,24},{32,40,48,56},{64,72,80,88},{96,104,112,120},{128,136,144,1..., dimensions={0} | all-to-all | bytes 1048576 | tf_op jit(solution)/shard_map/all_to_all | solution.py:407
  51.0 0.5 stage.1
  51.5 18.7 %all_to_all.27.got = bf16[16,32,128]{2,1,0:T(8,128)(2,1)S(1)} all-to-all(bf16[16,32,128]{2,1,0:T(8,128)(2,1)S(1)} %stage.1), channel_id=1, replica_groups={{0,32,64,96,128,160,192,224,256,288,320,352,384,416,448,480},{8,40,72,1..., dimensions={0} | all-to-all | bytes 262144 | tf_op jit(solution)/shard_map/all_to_all | solution.py:416
  70.2 0.3 combine.1
  70.5 13.9 %all_to_all.28 = bf16[8,2,896]{2,1,0:T(2,128)(2,1)S(1)} all-to-all(bf16[8,2,896]{2,1,0:T(2,128)(2,1)S(1)} %combine.1), channel_id=1, replica_groups=mesh['serve'=64,'tensor'=8] {'tensor'}, dimensions={0} | all-to-all | bytes 57344 | tf_op jit(solution)/shard_map/all_to_all | solution.py:425
  84.5 0.6 copy.10
Async XLA Ops:
  1.4 27.8 %all-to-all-start = ((bf16[16,32,128]{2,1,0:T(8,128)(2,1)}), bf16[16,32,128]{2,1,0:T(8,128)(2,1)S(1)}, u32[]{:S(2)}, u32[]{:S(2)}) async-start(bf16[16,32,128]{2,1,0:T(8,128)(2,1)} %prep.1), calls=%async_computation | async-start | bytes 262144 | tf_op jit(solution)/shard_map/all_to_all | solution.py:384
  29.2 11.3 %copy-start = (bf16[36,256,1,128]{3,1,2,0:T(8,128)(2,1)S(1)}, bf16[36,256,1,128]{3,1,2,0:T(8,128)(2,1)}, u32[]{:S(2)}) copy-start(bf16[36,256,1,128]{3,1,2,0:T(8,128)(2,1)} %param.11) | copy-start | bytes 7077892
  29.2 11.3 %copy-start.1 = (bf16[36,256,1,128]{3,1,2,0:T(8,128)(2,1)S(1)}, bf16[36,256,1,128]{3,1,2,0:T(8,128)(2,1)}, u32[]{:S(2)}) copy-start(bf16[36,256,1,128]{3,1,2,0:T(8,128)(2,1)} %param.12) | copy-start | bytes 7077892

commit v9 on v8

--- a/solution.py
+++ b/solution.py
@@ -18,8 +18,11 @@
     return lax.broadcasted_iota(jnp.int32, shape, dim)
 
 
+SIDE = 8
+
+
 def column_first(device):
-    return lax.bitwise_and(device, 3) * 16 + lax.shift_right_logical(device, 2)
+    return lax.bitwise_and(device, SIDE - 1) * SIDE + lax.shift_right_logical(device, 3)
 
 
 def message_of(out, lse, rows):
@@ -241,19 +244,26 @@
     sources, many, _, head_dim = got.shape
     rows = 28
     me = lax.axis_index("serve")
-    lse = gathered_lse([[got[k, m, PAD // 2 :, :] for k in range(sources)] for m in range(many)], rows)
-    top = four_fold(lse, jnp.maximum)
-    weight = jnp.exp2(lse - top)
-    total = four_fold(weight, jnp.add)
-    weight = weight / total
+    lse = [
+        gathered_lse(
+            [[got[k, m, PAD // 2 :, :] for k in range(first, first + 4)] for m in range(many)], rows
+        )
+        for first in range(0, sources, 4)
+    ]
+    top = four_fold(functools.reduce(jnp.maximum, lse), jnp.maximum)
+    weights = [jnp.exp2(part - top) for part in lse]
+    total = four_fold(sum(weights), jnp.add)
+    weights = [weight / total for weight in weights]
     row, lane = iota((PAD, head_dim), 0), iota((PAD, head_dim), 1)
     same = jnp.logical_and(lane % PAD == row, row < rows)
-    offset = lax.bitwise_and(lax.shift_right_logical(me, 2), 3) * PAD
+    offset = lax.bitwise_and(lax.shift_right_logical(me, 3), 3) * PAD
     lane = iota((many, head_dim), 1)
     in_span = jnp.logical_and(lane >= offset, lane < offset + rows)
     lse = jnp.where(in_span, top + jnp.log2(total), 0.0)
     for m in range(many):
-        spread = jnp.where(same, weight[m : m + 1], 0.0)
+        spread = jnp.concatenate(
+            [jnp.where(same, weight[m : m + 1], 0.0) for weight in weights], axis=1
+        )
         high = spread.astype(BF16)
         low = (spread - high.astype(F32)).astype(BF16)
         both = jnp.concatenate([high, low], axis=0)
@@ -324,8 +334,8 @@
     key_cache = key_cache.reshape(blocks, span, head_dim)
     value_cache = value_cache.reshape(blocks, span, head_dim)
 
-    along_z = [[4 * z + y for z in range(16)] for y in range(4)]
-    along_y = [[4 * z + y for y in range(4)] for z in range(16)]
+    outer = [[SIDE * k + m for k in range(SIDE)] for m in range(SIDE)]
+    inner = [[SIDE * k + m for m in range(SIDE)] for k in range(SIDE)]
     exchange = functools.partial(
         lax.all_to_all, axis_name="serve", split_axis=0, concat_axis=0, tiled=True
     )
@@ -340,7 +350,7 @@
     small = pltpu.CompilerParams(vmem_limit_bytes=8 << 20)
     message = pl.pallas_call(
         prep_kernel,
-        out_shape=jax.ShapeDtypeStruct((16, PAD, head_dim), BF16),
+        out_shape=jax.ShapeDtypeStruct((SIDE, PAD, head_dim), BF16),
         in_specs=[HBM, HBM],
         out_specs=VMEM,
         scratch_shapes=[
@@ -381,11 +391,11 @@
     )(
         lengths, block_owner, block_number, queries, new_keys, new_values, key_cache, value_cache
     )
-    column = exchange(message, axis_index_groups=along_z)
+    column = exchange(message, axis_index_groups=outer)
     column, local_out = lax.optimization_barrier((column, local_out))
     copies = pl.pallas_call(
         spread_kernel,
-        out_shape=jax.ShapeDtypeStruct((4,) + column.shape, BF16),
+        out_shape=jax.ShapeDtypeStruct((SIDE,) + column.shape, BF16),
         in_specs=[VMEM],
         out_specs=VMEM,
         compiler_params=small,
@@ -394,7 +404,7 @@
         ),
         name="spread",
     )(column)
-    far = exchange(copies, axis_index_groups=along_y)
+    far = exchange(copies, axis_index_groups=inner)
     back = pl.pallas_call(
         functools.partial(far_kernel, chunk, scale2),
         out_shape=jax.ShapeDtypeStruct((devices, PAD, head_dim), BF16),
@@ -403,17 +413,17 @@
         compiler_params=small,
         name="far",
     )(in_smem(table), far.reshape(devices, PAD, head_dim), in_vmem(plain_keys), in_vmem(plain_values))
-    back = back.reshape(4, 16, PAD, head_dim)
-    row_got = exchange(back, axis_index_groups=along_y)
+    back = back.reshape(SIDE, SIDE, PAD, head_dim)
+    row_got = exchange(back, axis_index_groups=inner)
     onward = pl.pallas_call(
         stage_kernel,
-        out_shape=jax.ShapeDtypeStruct((16, PAD, head_dim), BF16),
+        out_shape=jax.ShapeDtypeStruct((SIDE, PAD, head_dim), BF16),
         in_specs=[VMEM],
         out_specs=VMEM,
         compiler_params=small,
         name="stage",
     )(row_got)
-    got = exchange(onward, axis_index_groups=along_z)
+    got = exchange(onward, axis_index_groups=outer)
     rows_out = pl.pallas_call(
         combine_kernel,
         out_shape=jax.ShapeDtypeStruct((8, 2, groups * head_dim), BF16),

time: 85.6 us -> 84.2 us (0.984)
  blocking collectives: 53.1 us -> 51.7 us
    all_to_all x3, blocking collectives: 39.2 us -> 37.7 us  [the longest x1 16 us: shards(): got = exchange(onward, axis_index_groups=outer)]
where the time goes in v9:
time: 84.2 us; the launch traced here: 83.7 us
  blocking collectives  51.7 us (61%)
  starting transfers between devices  15.7 us (19%)
  waiting for transfers between devices  8.9 us (11%)
  Pallas kernels  6.79 us (8%)
    all_to_all x1, blocking collectives, shards(): got = exchange(onward, axis_index_groups=outer)  16 us
    all_to_all x1, starting transfers between devices, shards(): column = exchange(message, axis_index_groups=outer)  15.7 us
    all_to_all x1, blocking collectives, shards(): lax.all_to_all(rows_out, 'tensor', split_axis=0, concat_axis=0, tiled=True)  14 us
    all_to_all x1, blocking collectives, shards(): far = exchange(copies, axis_index_groups=inner)  11.8 us
    all_to_all x1, blocking collectives, shards(): row_got = exchange(back, axis_index_groups=inner)  9.89 us
    all_to_all x1, waiting for transfers between devices, shards(): column = exchange(message, axis_index_groups=outer)  8.9 us
    pallas_call x1, Pallas kernels, shards(): pl.pallas_call(functools.partial(local_kernel, scale2), out_shape=(pltpu....  3.29 us
  transfers between devices with their start and end apart: 1, of which 1 were waited for; matrix products, arithmetic and copies ran while one was open for 0% of the time, Pallas kernels for 4%

profile of v9, /device:TPU:1, one launch (start us, length us, event | category | flops | bytes accessed | tf_op | source)
XLA Modules:
  0.0 83.7 jit_solution(11648316715385155017)
XLA Ops:
  0.0 1.4 %prep.1 = bf16[8,32,128]{2,1,0:T(8,128)(2,1)} custom-call(s32[4]{0:T(128)} %lengths_hbm.3, bf16[4,7,4,128]{3,2,1,0:T(4,128)(2,1)} %bitcast.16), custom_call_target="tpu_custom_call" | custom-call | tf_op jit(solution)/shard_map/prep/pallas_call | solution.py:351
  1.4 15.7 %all-to-all-start = ((bf16[8,32,128]{2,1,0:T(8,128)(2,1)}), bf16[8,32,128]{2,1,0:T(8,128)(2,1)S(1)}, u32[]{:S(2)}, u32[]{:S(2)}) async-start(bf16[8,32,128]{2,1,0:T(8,128)(2,1)} %prep.1), calls=%async_computation | async-start | bytes 131072 | tf_op jit(solution)/shard_map/all_to_all | solution.py:394
  17.1 3.3 %local.1 = (s32[256]{0:T(256)S(4)}, f32[4,32,128]{2,1,0:T(8,128)S(1)}, f32[4,32,128]{2,1,0:T(8,128)S(1)}) custom-call(s32[4]{0:T(128)} %lengths_hbm.3, s32[36]{0:T(128)} %owners_hbm.1, s32[36]{0:T(128)} %numbers_hbm.1, bf16[4,7,4,128]{3,2,1,0:T(4,128)(2,1)} %bitcast.17, bf16[4,4,128]{2,1,0:T(4,128)(2,1)} %bitcast.19, bf16[4,4,128]{2,1,0:T(4,128)(2,1)} %bitcast.20, ...), custom_call_target="tpu_custom_call" | custom-call | flops 268435456 | bytes 2359296 | tf_op jit(solution)/shard_map/local/pallas_call | solution.py:365
  20.4 8.9 %all-to-all-done.column = bf16[8,32,128]{2,1,0:T(8,128)(2,1)S(1)} async-done(((bf16[8,32,128]{2,1,0:T(8,128)(2,1)}), bf16[8,32,128]{2,1,0:T(8,128)(2,1)S(1)}, u32[]{:S(2)}, u32[]{:S(2)}) %all-to-all-start) | async-done | bytes 65568 | tf_op jit(solution)/shard_map/all_to_all | solution.py:394
  29.3 0.0 copy-start
  29.3 0.0 copy-start.1
  29.3 0.1 spread.1
  29.3 11.8 %all_to_all.25 = bf16[8,8,32,128]{3,2,1,0:T(8,128)(2,1)S(1)} all-to-all(bf16[8,8,32,128]{3,2,1,0:T(8,128)(2,1)S(1)} %spread.1), channel_id=1, replica_groups={{0,8,16,24,32,40,48,56},{64,72,80,88,96,104,112,120},{128,136,144,152,1..., dimensions={0} | all-to-all | bytes 1048576 | tf_op jit(solution)/shard_map/all_to_all | solution.py:407
  41.2 0.0 copy-done
  41.2 0.0 copy-done.1
  41.2 1.2 %far.1 = bf16[64,32,128]{2,1,0:T(8,128)(2,1)S(1)} custom-call(s32[256]{0:T(256)S(4)} %get-tuple-element.10.table, bf16[64,32,128]{2,1,0:T(8,128)(2,1)S(1)} %bitcast.14, bf16[36,256,128]{2,1,0:T(8,128)(2,1)S(1)} %bitcast.11, bf16[36,256,128]{2,1,0:T(8,128)(2,1)S(1)} %bitcast.13), custom_call_target="tpu_custom_call" | custom-call | tf_op jit(solution)/shard_map/far/pallas_call | solution.py:408
  42.4 9.9 %all_to_all.26.got = bf16[8,8,32,128]{3,2,1,0:T(8,128)(2,1)S(1)} all-to-all(bf16[8,8,32,128]{3,2,1,0:T(8,128)(2,1)S(1)} %bitcast.15), channel_id=1, replica_groups={{0,8,16,24,32,40,48,56},{64,72,80,88,96,104,112,120},{128,136,144,152,1..., dimensions={0} | all-to-all | bytes 1048576 | tf_op jit(solution)/shard_map/all_to_all | solution.py:417
  52.3 0.5 stage.1
  52.8 16.0 %all_to_all.27.got = bf16[8,32,128]{2,1,0:T(8,128)(2,1)S(1)} all-to-all(bf16[8,32,128]{2,1,0:T(8,128)(2,1)S(1)} %stage.1), channel_id=1, replica_groups={{0,64,128,192,256,320,384,448},{8,72,136,200,264,328,392,456},{16,80,14..., dimensions={0} | all-to-all | bytes 131072 | tf_op jit(solution)/shard_map/all_to_all | solution.py:426
  68.8 0.3 combine.1
  69.1 14.0 %all_to_all.28 = bf16[8,2,896]{2,1,0:T(2,128)(2,1)S(1)} all-to-all(bf16[8,2,896]{2,1,0:T(2,128)(2,1)S(1)} %combine.1), channel_id=1, replica_groups=mesh['serve'=64,'tensor'=8] {'tensor'}, dimensions={0} | all-to-all | bytes 57344 | tf_op jit(solution)/shard_map/all_to_all | solution.py:435
  83.1 0.6 copy.10
Async XLA Ops:
  1.4 27.9 %all-to-all-start = ((bf16[8,32,128]{2,1,0:T(8,128)(2,1)}), bf16[8,32,128]{2,1,0:T(8,128)(2,1)S(1)}, u32[]{:S(2)}, u32[]{:S(2)}) async-start(bf16[8,32,128]{2,1,0:T(8,128)(2,1)} %prep.1), calls=%async_computation | async-start | bytes 131072 | tf_op jit(solution)/shard_map/all_to_all | solution.py:394
  29.3 11.9 %copy-start = (bf16[36,256,1,128]{3,1,2,0:T(8,128)(2,1)S(1)}, bf16[36,256,1,128]{3,1,2,0:T(8,128)(2,1)}, u32[]{:S(2)}) copy-start(bf16[36,256,1,128]{3,1,2,0:T(8,128)(2,1)} %param.11) | copy-start | bytes 7077892
  29.3 11.9 %copy-start.1 = (bf16[36,256,1,128]{3,1,2,0:T(8,128)(2,1)S(1)}, bf16[36,256,1,128]{3,1,2,0:T(8,128)(2,1)}, u32[]{:S(2)}) copy-start(bf16[36,256,1,128]{3,1,2,0:T(8,128)(2,1)} %param.12) | copy-start | bytes 7077892

commit v10 on v9

--- a/solution.py
+++ b/solution.py
@@ -73,14 +73,18 @@
     message[...] = jnp.broadcast_to(padded[...].astype(BF16)[None], message.shape)
 
 
-def attend(query, limit, keys, values, scale2):
+def weigh(query, limit, keys, scale2):
     score = lax.dot_general(query, keys, (((1,), (1,)), ((), ())), preferred_element_type=F32)
     score = jnp.where(iota(score.shape, 1).astype(F32) < limit, score, neg_fill)
     top = jnp.max(score, axis=1, keepdims=True)
     weights = jnp.exp2((score - top) * scale2).astype(BF16)
     total = jnp.sum(weights.astype(F32), axis=1, keepdims=True)
+    return weights, total, top * scale2 + jnp.log2(total)
+
+
+def apply(weights, total, values):
     out = lax.dot_general(weights, values, (((1,), (0,)), ((), ())), preferred_element_type=F32)
-    return out / total, top * scale2 + jnp.log2(total)
+    return out / total
 
 
 def local_kernel(
@@ -143,18 +147,19 @@
         local_out[slot] = (a * local_out[slot] + b * new_out) / total
         local_lse[slot] = overall + jnp.log2(total)
 
-    for copy in own_blocks:
+    for copy in own_blocks[:slots]:
         copy.wait()
     ats = [blocks - 1 - k for k in range(slots)]
     parts = []
     for k, at in enumerate(ats):
         slot = table[64 + at]
         limit = (lengths[slot] - table[128 + at]).astype(F32)
-        parts.append(
-            attend(padded[slot].astype(BF16), limit, near_keys[k], near_values[k], scale2)
-        )
-    for at, (new_out, new) in zip(ats, parts):
-        merge(table[64 + at], new_out, jnp.broadcast_to(new, new_out.shape))
+        parts.append(weigh(padded[slot].astype(BF16), limit, near_keys[k], scale2))
+    for copy in own_blocks[slots:]:
+        copy.wait()
+    outs = [apply(part[0], part[1], near_values[k]) for k, part in enumerate(parts)]
+    for at, part, new_out in zip(ats, parts, outs):
+        merge(table[64 + at], new_out, jnp.broadcast_to(part[2], new_out.shape))
 
     def more(k, carry):
         at = blocks - 1 - k
@@ -164,9 +169,8 @@
         for copy in fetch(pair, sems.at[pl.ds(8, 2)]):
             copy.wait()
         limit = (lengths[slot] - table[128 + at]).astype(F32)
-        new_out, new = attend(
-            padded[slot].astype(BF16), limit, near_keys[0], near_values[0], scale2
-        )
+        weights, total, new = weigh(padded[slot].astype(BF16), limit, near_keys[0], scale2)
+        new_out = apply(weights, total, near_values[0])
         merge(slot, new_out, jnp.broadcast_to(new, new_out.shape))
         return carry
 

time: 84.2 us -> 84.2 us (level)
  transfers between devices with their start and end apart: 1 -> 1, of which waited for: 1 -> 1; matrix products, arithmetic and copies ran while one was open for 0% -> 0% of each run, Pallas kernels for 4% -> 3%
where the time goes in v10:
time: 84.2 us; the launch traced here: 83.7 us
  blocking collectives  51.7 us (61%)
  starting transfers between devices  15.7 us (19%)
  waiting for transfers between devices  9.54 us (11%)
  Pallas kernels  6.15 us (7%)
    all_to_all x1, blocking collectives, shards(): got = exchange(onward, axis_index_groups=outer)  16 us
    all_to_all x1, starting transfers between devices, shards(): column = exchange(message, axis_index_groups=outer)  15.7 us
    all_to_all x1, blocking collectives, shards(): lax.all_to_all(rows_out, 'tensor', split_axis=0, concat_axis=0, tiled=True)  14 us
    all_to_all x1, blocking collectives, shards(): far = exchange(copies, axis_index_groups=inner)  11.8 us
    all_to_all x1, blocking collectives, shards(): row_got = exchange(back, axis_index_groups=inner)  9.89 us
    all_to_all x1, waiting for transfers between devices, shards(): column = exchange(message, axis_index_groups=outer)  9.54 us
    pallas_call x1, Pallas kernels, shards(): pl.pallas_call(functools.partial(local_kernel, scale2), out_shape=(pltpu....  2.65 us
  transfers between devices with their start and end apart: 1, of which 1 were waited for; matrix products, arithmetic and copies ran while one was open for 0% of the time, Pallas kernels for 3%

profile of v10, /device:TPU:1, one launch (start us, length us, event | category | flops | bytes accessed | tf_op | source)
XLA Modules:
  0.0 83.7 jit_solution(11581139134514452088)
XLA Ops:
  0.0 1.4 %prep.1 = bf16[8,32,128]{2,1,0:T(8,128)(2,1)} custom-call(s32[4]{0:T(128)} %lengths_hbm.3, bf16[4,7,4,128]{3,2,1,0:T(4,128)(2,1)} %bitcast.16), custom_call_target="tpu_custom_call" | custom-call | tf_op jit(solution)/shard_map/prep/pallas_call | solution.py:355
  1.4 15.7 %all-to-all-start = ((bf16[8,32,128]{2,1,0:T(8,128)(2,1)}), bf16[8,32,128]{2,1,0:T(8,128)(2,1)S(1)}, u32[]{:S(2)}, u32[]{:S(2)}) async-start(bf16[8,32,128]{2,1,0:T(8,128)(2,1)} %prep.1), calls=%async_computation | async-start | bytes 131072 | tf_op jit(solution)/shard_map/all_to_all | solution.py:398
  17.1 2.7 %local.1 = (s32[256]{0:T(256)S(4)}, f32[4,32,128]{2,1,0:T(8,128)S(1)}, f32[4,32,128]{2,1,0:T(8,128)S(1)}) custom-call(s32[4]{0:T(128)} %lengths_hbm.3, s32[36]{0:T(128)} %owners_hbm.1, s32[36]{0:T(128)} %numbers_hbm.1, bf16[4,7,4,128]{3,2,1,0:T(4,128)(2,1)} %bitcast.17, bf16[4,4,128]{2,1,0:T(4,128)(2,1)} %bitcast.19, bf16[4,4,128]{2,1,0:T(4,128)(2,1)} %bitcast.20, ...), custom_call_target="tpu_custom_call" | custom-call | flops 268435456 | bytes 2359296 | tf_op jit(solution)/shard_map/local/pallas_call | solution.py:369
  19.7 9.5 %all-to-all-done.column = bf16[8,32,128]{2,1,0:T(8,128)(2,1)S(1)} async-done(((bf16[8,32,128]{2,1,0:T(8,128)(2,1)}), bf16[8,32,128]{2,1,0:T(8,128)(2,1)S(1)}, u32[]{:S(2)}, u32[]{:S(2)}) %all-to-all-start) | async-done | bytes 65568 | tf_op jit(solution)/shard_map/all_to_all | solution.py:398
  29.3 0.0 copy-start
  29.3 0.0 copy-start.1
  29.3 0.1 spread.1
  29.3 11.8 %all_to_all.25 = bf16[8,8,32,128]{3,2,1,0:T(8,128)(2,1)S(1)} all-to-all(bf16[8,8,32,128]{3,2,1,0:T(8,128)(2,1)S(1)} %spread.1), channel_id=1, replica_groups={{0,8,16,24,32,40,48,56},{64,72,80,88,96,104,112,120},{128,136,144,152,1..., dimensions={0} | all-to-all | bytes 1048576 | tf_op jit(solution)/shard_map/all_to_all | solution.py:411
  41.2 0.0 copy-done
  41.2 0.0 copy-done.1
  41.2 1.2 %far.1 = bf16[64,32,128]{2,1,0:T(8,128)(2,1)S(1)} custom-call(s32[256]{0:T(256)S(4)} %get-tuple-element.10.table, bf16[64,32,128]{2,1,0:T(8,128)(2,1)S(1)} %bitcast.14, bf16[36,256,128]{2,1,0:T(8,128)(2,1)S(1)} %bitcast.11, bf16[36,256,128]{2,1,0:T(8,128)(2,1)S(1)} %bitcast.13), custom_call_target="tpu_custom_call" | custom-call | tf_op jit(solution)/shard_map/far/pallas_call | solution.py:412
  42.4 9.9 %all_to_all.26.got = bf16[8,8,32,128]{3,2,1,0:T(8,128)(2,1)S(1)} all-to-all(bf16[8,8,32,128]{3,2,1,0:T(8,128)(2,1)S(1)} %bitcast.15), channel_id=1, replica_groups={{0,8,16,24,32,40,48,56},{64,72,80,88,96,104,112,120},{128,136,144,152,1..., dimensions={0} | all-to-all | bytes 1048576 | tf_op jit(solution)/shard_map/all_to_all | solution.py:421
  52.3 0.5 stage.1
  52.8 16.0 %all_to_all.27.got = bf16[8,32,128]{2,1,0:T(8,128)(2,1)S(1)} all-to-all(bf16[8,32,128]{2,1,0:T(8,128)(2,1)S(1)} %stage.1), channel_id=1, replica_groups={{0,64,128,192,256,320,384,448},{8,72,136,200,264,328,392,456},{16,80,14..., dimensions={0} | all-to-all | bytes 131072 | tf_op jit(solution)/shard_map/all_to_all | solution.py:430
  68.8 0.3 combine.1
  69.1 14.0 %all_to_all.28 = bf16[8,2,896]{2,1,0:T(2,128)(2,1)S(1)} all-to-all(bf16[8,2,896]{2,1,0:T(2,128)(2,1)S(1)} %combine.1), channel_id=1, replica_groups=mesh['serve'=64,'tensor'=8] {'tensor'}, dimensions={0} | all-to-all | bytes 57344 | tf_op jit(solution)/shard_map/all_to_all | solution.py:439
  83.1 0.6 copy.10
Async XLA Ops:
  1.4 27.9 %all-to-all-start = ((bf16[8,32,128]{2,1,0:T(8,128)(2,1)}), bf16[8,32,128]{2,1,0:T(8,128)(2,1)S(1)}, u32[]{:S(2)}, u32[]{:S(2)}) async-start(bf16[8,32,128]{2,1,0:T(8,128)(2,1)} %prep.1), calls=%async_computation | async-start | bytes 131072 | tf_op jit(solution)/shard_map/all_to_all | solution.py:398
  29.3 11.9 %copy-start = (bf16[36,256,1,128]{3,1,2,0:T(8,128)(2,1)S(1)}, bf16[36,256,1,128]{3,1,2,0:T(8,128)(2,1)}, u32[]{:S(2)}) copy-start(bf16[36,256,1,128]{3,1,2,0:T(8,128)(2,1)} %param.11) | copy-start | bytes 7077892
  29.3 11.9 %copy-start.1 = (bf16[36,256,1,128]{3,1,2,0:T(8,128)(2,1)S(1)}, bf16[36,256,1,128]{3,1,2,0:T(8,128)(2,1)}, u32[]{:S(2)}) copy-start(bf16[36,256,1,128]{3,1,2,0:T(8,128)(2,1)} %param.12) | copy-start | bytes 7077892

commit v11 on v10

--- a/solution.py
+++ b/solution.py
@@ -268,12 +268,11 @@
         spread = jnp.concatenate(
             [jnp.where(same, weight[m : m + 1], 0.0) for weight in weights], axis=1
         )
-        high = spread.astype(BF16)
-        low = (spread - high.astype(F32)).astype(BF16)
-        both = jnp.concatenate([high, low], axis=0)
         block = got[:, m].reshape(sources * PAD, head_dim)
-        out = lax.dot_general(both, block, (((1,), (0,)), ((), ())), preferred_element_type=F32)
-        onward[m] = message_of(out[:PAD] + out[PAD:], lse[m : m + 1], rows)
+        out = lax.dot_general(
+            spread.astype(BF16), block, (((1,), (0,)), ((), ())), preferred_element_type=F32
+        )
+        onward[m] = message_of(out, lse[m : m + 1], rows)
 
 
 def combine_kernel(table, got, local_out, local_lse, result):

time: 84.2 us -> 84.2 us (level)
  no operation moved by 1% of the time
where the time goes in v11:
time: 84.2 us; the launch traced here: 83.7 us
  blocking collectives  51.7 us (61%)
  starting transfers between devices  15.7 us (19%)
  waiting for transfers between devices  9.54 us (11%)
  Pallas kernels  6.13 us (7%)
    all_to_all x1, blocking collectives, shards(): got = exchange(onward, axis_index_groups=outer)  16 us
    all_to_all x1, starting transfers between devices, shards(): column = exchange(message, axis_index_groups=outer)  15.7 us
    all_to_all x1, blocking collectives, shards(): lax.all_to_all(rows_out, 'tensor', split_axis=0, concat_axis=0, tiled=True)  14 us
    all_to_all x1, blocking collectives, shards(): far = exchange(copies, axis_index_groups=inner)  11.8 us
    all_to_all x1, blocking collectives, shards(): row_got = exchange(back, axis_index_groups=inner)  9.89 us
    all_to_all x1, waiting for transfers between devices, shards(): column = exchange(message, axis_index_groups=outer)  9.54 us
    pallas_call x1, Pallas kernels, shards(): pl.pallas_call(functools.partial(local_kernel, scale2), out_shape=(pltpu....  2.65 us
  transfers between devices with their start and end apart: 1, of which 1 were waited for; matrix products, arithmetic and copies ran while one was open for 0% of the time, Pallas kernels for 3%

profile of v11, /device:TPU:1, one launch (start us, length us, event | category | flops | bytes accessed | tf_op | source)
XLA Modules:
  0.0 83.7 jit_solution(11413352160540666632)
XLA Ops:
  0.0 1.4 %prep.1 = bf16[8,32,128]{2,1,0:T(8,128)(2,1)} custom-call(s32[4]{0:T(128)} %lengths_hbm.3, bf16[4,7,4,128]{3,2,1,0:T(4,128)(2,1)} %bitcast.16), custom_call_target="tpu_custom_call" | custom-call | tf_op jit(solution)/shard_map/prep/pallas_call | solution.py:354
  1.4 15.7 %all-to-all-start = ((bf16[8,32,128]{2,1,0:T(8,128)(2,1)}), bf16[8,32,128]{2,1,0:T(8,128)(2,1)S(1)}, u32[]{:S(2)}, u32[]{:S(2)}) async-start(bf16[8,32,128]{2,1,0:T(8,128)(2,1)} %prep.1), calls=%async_computation | async-start | bytes 131072 | tf_op jit(solution)/shard_map/all_to_all | solution.py:397
  17.1 2.7 %local.1 = (s32[256]{0:T(256)S(4)}, f32[4,32,128]{2,1,0:T(8,128)S(1)}, f32[4,32,128]{2,1,0:T(8,128)S(1)}) custom-call(s32[4]{0:T(128)} %lengths_hbm.3, s32[36]{0:T(128)} %owners_hbm.1, s32[36]{0:T(128)} %numbers_hbm.1, bf16[4,7,4,128]{3,2,1,0:T(4,128)(2,1)} %bitcast.17, bf16[4,4,128]{2,1,0:T(4,128)(2,1)} %bitcast.19, bf16[4,4,128]{2,1,0:T(4,128)(2,1)} %bitcast.20, ...), custom_call_target="tpu_custom_call" | custom-call | flops 268435456 | bytes 2359296 | tf_op jit(solution)/shard_map/local/pallas_call | solution.py:368
  19.7 9.5 %all-to-all-done.column = bf16[8,32,128]{2,1,0:T(8,128)(2,1)S(1)} async-done(((bf16[8,32,128]{2,1,0:T(8,128)(2,1)}), bf16[8,32,128]{2,1,0:T(8,128)(2,1)S(1)}, u32[]{:S(2)}, u32[]{:S(2)}) %all-to-all-start) | async-done | bytes 65568 | tf_op jit(solution)/shard_map/all_to_all | solution.py:397
  29.3 0.0 copy-start
  29.3 0.0 copy-start.1
  29.3 0.1 spread.1
  29.3 11.8 %all_to_all.25 = bf16[8,8,32,128]{3,2,1,0:T(8,128)(2,1)S(1)} all-to-all(bf16[8,8,32,128]{3,2,1,0:T(8,128)(2,1)S(1)} %spread.1), channel_id=1, replica_groups={{0,8,16,24,32,40,48,56},{64,72,80,88,96,104,112,120},{128,136,144,152,1..., dimensions={0} | all-to-all | bytes 1048576 | tf_op jit(solution)/shard_map/all_to_all | solution.py:410
  41.2 0.0 copy-done
  41.2 0.0 copy-done.1
  41.2 1.2 %far.1 = bf16[64,32,128]{2,1,0:T(8,128)(2,1)S(1)} custom-call(s32[256]{0:T(256)S(4)} %get-tuple-element.10.table, bf16[64,32,128]{2,1,0:T(8,128)(2,1)S(1)} %bitcast.14, bf16[36,256,128]{2,1,0:T(8,128)(2,1)S(1)} %bitcast.11, bf16[36,256,128]{2,1,0:T(8,128)(2,1)S(1)} %bitcast.13), custom_call_target="tpu_custom_call" | custom-call | tf_op jit(solution)/shard_map/far/pallas_call | solution.py:411
  42.4 9.9 %all_to_all.26.got = bf16[8,8,32,128]{3,2,1,0:T(8,128)(2,1)S(1)} all-to-all(bf16[8,8,32,128]{3,2,1,0:T(8,128)(2,1)S(1)} %bitcast.15), channel_id=1, replica_groups={{0,8,16,24,32,40,48,56},{64,72,80,88,96,104,112,120},{128,136,144,152,1..., dimensions={0} | all-to-all | bytes 1048576 | tf_op jit(solution)/shard_map/all_to_all | solution.py:420
  52.3 0.5 stage.1
  52.8 16.0 %all_to_all.27.got = bf16[8,32,128]{2,1,0:T(8,128)(2,1)S(1)} all-to-all(bf16[8,32,128]{2,1,0:T(8,128)(2,1)S(1)} %stage.1), channel_id=1, replica_groups={{0,64,128,192,256,320,384,448},{8,72,136,200,264,328,392,456},{16,80,14..., dimensions={0} | all-to-all | bytes 131072 | tf_op jit(solution)/shard_map/all_to_all | solution.py:429
  68.8 0.3 combine.1
  69.1 14.0 %all_to_all.28 = bf16[8,2,896]{2,1,0:T(2,128)(2,1)S(1)} all-to-all(bf16[8,2,896]{2,1,0:T(2,128)(2,1)S(1)} %combine.1), channel_id=1, replica_groups=mesh['serve'=64,'tensor'=8] {'tensor'}, dimensions={0} | all-to-all | bytes 57344 | tf_op jit(solution)/shard_map/all_to_all | solution.py:438
  83.1 0.6 copy.10
Async XLA Ops:
  1.4 27.9 %all-to-all-start = ((bf16[8,32,128]{2,1,0:T(8,128)(2,1)}), bf16[8,32,128]{2,1,0:T(8,128)(2,1)S(1)}, u32[]{:S(2)}, u32[]{:S(2)}) async-start(bf16[8,32,128]{2,1,0:T(8,128)(2,1)} %prep.1), calls=%async_computation | async-start | bytes 131072 | tf_op jit(solution)/shard_map/all_to_all | solution.py:397
  29.3 11.9 %copy-start = (bf16[36,256,1,128]{3,1,2,0:T(8,128)(2,1)S(1)}, bf16[36,256,1,128]{3,1,2,0:T(8,128)(2,1)}, u32[]{:S(2)}) copy-start(bf16[36,256,1,128]{3,1,2,0:T(8,128)(2,1)} %param.11) | copy-start | bytes 7077892
  29.3 11.9 %copy-start.1 = (bf16[36,256,1,128]{3,1,2,0:T(8,128)(2,1)S(1)}, bf16[36,256,1,128]{3,1,2,0:T(8,128)(2,1)}, u32[]{:S(2)}) copy-start(bf16[36,256,1,128]{3,1,2,0:T(8,128)(2,1)} %param.12) | copy-start | bytes 7077892
